TPU v7x, 512 devices: a whole 4x4x16 slice. The times are simulated.
512 devices in a mesh: bins: 64 (over z, y), freq: 8 (over x, core).
Axes of the slice: x: 4, y: 4, z: 16, core: 2. Of those that a mesh axis runs over, the one named last changes fastest.
Arguments:
- traces: bfloat16 [2000, 524288], P('freq', 'bins'), may hold values from -6 to 6
- bin_ids: int32 [524288], P('bins'), may hold values from 0 to 1023
- valid: int32 [524288], P('bins'), may hold values 0 or 1
- tile_owner: int32 [4096, 1], P('bins'), may hold values from 0 to 63; in each aligned block of 64 rows (0 to 63, 64 to 127, ...) at most 2 rows name the same one
Outputs:
- rebuilt: float32 [512, 2, 65536], P(('bins', 'freq'))
Inputs may be any that keep to these rules, and one draw needn't show every extreme that they name: `tile_owner`: within the tiles of one shot group (aligned blocks of 64 tiles) no owner is named by more than 2 tiles.
All inputs are finite; a program needn't handle non-finite values. No bound on the sum of `valid` on one device may be relied on, other than what follows from the above.
Results may differ from a plain program's by a relative error of at most 0.0038.
Values may be sent and summed in bfloat16 or wider, within the bound.
A program may use at most 128 MiB of HBM per device.

v0:
```python
import math

import jax
import jax.numpy as jnp
from jax import lax
from jax.sharding import PartitionSpec as P

MX = 16
MY = 16
HX = 16
HY = 16
FREQ_DEV = 1
ITERS = 2


def time_table(freq_index, times, total):
    phase = (freq_index[None, :] + 1) * times[:, None] % total
    angle = phase.astype(jnp.float32) * (2.0 * math.pi / total)
    norm = 1.0 / math.sqrt(total)
    table = jnp.stack([jnp.cos(angle) * norm, -jnp.sin(angle) * norm], axis=2)
    return table.reshape(times.shape[0], -1).astype(jnp.bfloat16)


def slice_rows(rows, per_group, groups):
    member = rows // per_group
    within = rows % per_group
    return (within // FREQ_DEV * groups + member) * FREQ_DEV + within % FREQ_DEV


def pair_table(first, second, sign):
    index = jnp.arange(first * second, dtype=jnp.int32)
    major = index // second
    minor = index % second
    phase = (major[:, None] * major[None, :] % first).astype(jnp.float32) / first
    phase = phase + (minor[:, None] * minor[None, :] % second).astype(jnp.float32) / second
    angle = phase * (2.0 * math.pi)
    return (jnp.cos(angle), sign * jnp.sin(angle))


def exact_dot(left, right):
    return jnp.dot(left, right, precision=lax.Precision.HIGHEST, preferred_element_type=jnp.float32)


def paired_transform(real, imag, sign):
    left_cos, left_sin = pair_table(MX, MY, sign)
    right_cos, right_sin = pair_table(HX, HY, sign)
    real = real.reshape(MX * MY, HX * HY)
    imag = imag.reshape(MX * MY, HX * HY)
    mid_re = exact_dot(left_cos, real) - exact_dot(left_sin, imag)
    mid_im = exact_dot(left_cos, imag) + exact_dot(left_sin, real)
    out_re = exact_dot(mid_re, right_cos) - exact_dot(mid_im, right_sin)
    out_im = exact_dot(mid_re, right_sin) + exact_dot(mid_im, right_cos)
    return (out_re.reshape(-1), out_im.reshape(-1))


def grid_transform(real, imag, sign):
    return paired_transform(real, imag, sign)


def local(traces, bin_ids, valid, tile_owner):
    owners = lax.axis_size("bins")
    groups = lax.axis_size("freq")
    tiles_dev = tile_owner.shape[0]
    tile_len = traces.shape[1] // tiles_dev
    span = traces.shape[0]
    cells = MX * MY * HX * HY
    local_bins = cells // owners
    capacity = max(2, (2 * tiles_dev + owners - 1) // owners)
    owner = tile_owner[:, 0]
    hits = (owner[:, None] == jnp.arange(owners, dtype=jnp.int32)[None, :]).astype(jnp.int32)
    earlier = jnp.cumsum(hits, axis=0) - hits
    rank = jnp.sum(earlier * hits, axis=1)
    position = owner * capacity + rank
    labels = jnp.where(valid > 0, bin_ids, local_bins).reshape(tiles_dev, tile_len)
    data_buf = (
        jnp.zeros((span, owners * capacity, tile_len), jnp.bfloat16)
        .at[:, position]
        .set(traces.reshape(span, tiles_dev, tile_len))
    )
    label_buf = (
        jnp.full((owners * capacity, tile_len), local_bins, jnp.int32).at[position].set(labels)
    )
    arrived, arrived_labels = (
        lax.all_to_all(
            data_buf.reshape(span, owners, capacity * tile_len),
            "bins",
            split_axis=1,
            concat_axis=1,
            tiled=True,
        ),
        lax.all_to_all(
            label_buf.reshape(1, owners, capacity * tile_len),
            "bins",
            split_axis=1,
            concat_axis=1,
            tiled=True,
        ),
    )
    flat_labels = arrived_labels.reshape(-1)
    columns = arrived.reshape(span, -1).T.astype(jnp.float32)
    sums = jax.ops.segment_sum(columns, flat_labels, local_bins + 1)[:local_bins]
    count = jax.ops.segment_sum(
        jnp.ones(flat_labels.shape, jnp.float32), flat_labels, local_bins + 1
    )[:local_bins]
    binned = (sums / jnp.maximum(count, 1.0)[:, None]).astype(jnp.bfloat16)
    total_len = span * groups
    per_group = FREQ_DEV * owners
    contract = (((0,), (1,)), ((), ()))
    times = lax.axis_index("freq") * span + jnp.arange(span, dtype=jnp.int32)
    rows = jnp.arange(lax.axis_size("freq") * per_group, dtype=jnp.int32)
    table = time_table(slice_rows(rows, per_group, groups), times, total_len)
    part = lax.dot_general(table, binned, contract, preferred_element_type=jnp.float32)
    spectra = lax.psum_scatter(
        part.reshape(lax.axis_size("freq") * per_group, 2, local_bins),
        "freq",
        scatter_dimension=0,
        tiled=True,
    )
    fields = lax.all_to_all(spectra, "bins", split_axis=0, concat_axis=2, tiled=True)
    coverage = lax.all_gather(
        jnp.minimum(count, 1.0).astype(jnp.bfloat16), "bins", axis=0, tiled=True
    ).astype(jnp.float32)
    observed = fields[0]
    state = observed
    for step in range(ITERS):
        mixed = coverage * observed + (1.0 - coverage) * state
        spec_re, spec_im = grid_transform(mixed[0], mixed[1], -1.0)
        power = spec_re * spec_re + spec_im * spec_im
        damping = 0.5 * jnp.mean(power) + 1e-06
        keep = power / (power + damping)
        back_re, back_im = grid_transform(spec_re * keep, spec_im * keep, 1.0)
        state = jnp.stack([back_re, back_im]) / cells
    results = [state]
    return jnp.stack(results)


def solution(mesh):
    in_specs = (P("freq", "bins"), P("bins"), P("bins"), P("bins", None))
    out_specs = P(("bins", "freq"), None, None)
    return jax.shard_map(local, mesh=mesh, in_specs=in_specs, out_specs=out_specs, check_vma=False)
```

profile of v0, /device:TPU:6, one launch (start us, length us, event | category | flops | bytes accessed | tf_op | source)
XLA Modules:
  0.0 797.1 jit_solution(18017370393931948517)
XLA Ops:
  6.5 0.7 fusion.95
  7.4 0.8 select_reduce_fusion
  8.2 0.7 fusion.114
  8.9 1.6 scatter_custom_fusion
  10.4 18.7 %all-to-all-start = ((s32[1,64,256]{2,0,1:T(1,128)}), s32[1,64,256]{2,0,1:T(1,128)S(1)}, u32[]{:S(2)}, u32[]{:S(2)}) async-start(s32[1,64,256]{2,0,1:T(1,128)} %bitcast.4), calls=%async_computation | async-start | bytes 131072 | tf_op jit(solution)/shard_map/all_to_all | solution.py:91
  29.2 3.4 copy.13
  32.6 0.9 slice.30
  33.5 4.6 copy.19
  38.1 5.3 broadcast_in_dim.19
  43.4 11.9 %scatter_fusion = bf16[250,128,128]{2,0,1:T(8,128)(2,1)} fusion(bf16[250,128,128]{2,0,1:T(8,128)(2,1)} %broadcast_in_dim.19, s32[64]{0:T(128)S(1)} %fusion.114, bf16[64,250,128]{2,1,0:T(8,128)(2,1)} %bitcast.68), kind=kCustom, calls=%fused_computation.2 | custom fusion | bytes 12288256 | tf_op jit(solution)/shard_map/scatter | solution.py:78
  55.4 11.9 %copy.10 = bf16[250,128,128]{0,2,1:T(8,128)(2,1)} copy(bf16[250,128,128]{2,0,1:T(8,128)(2,1)} %scatter_fusion) | data formatting | bytes 16384000 | tf_op jit(solution)/shard_map/scatter | solution.py:78
  67.3 15.3 %all-to-all-start.1 = ((bf16[250,64,256]{0,2,1:T(8,128)(2,1)}), bf16[250,64,256]{0,2,1:T(8,128)(2,1)}, u32[]{:S(2)}, u32[]{:S(2)}) async-start(bf16[250,64,256]{0,2,1:T(8,128)(2,1)} %bitcast.67), calls=%async_computation.1 | async-start | bytes 16777216 | tf_op jit(solution)/shard_map/all_to_all | solution.py:84
  82.8 18.4 %multiply_convert_fusion.1 = (bf16[250,512,1]{0,2,1:T(2,128)(2,1)S(1)}, bf16[250,512,1]{0,2,1:T(2,128)(2,1)S(1)}) fusion(s32[250]{0:T(256)S(1)} %iota_add_fusion, s32[512]{0:T(512)S(1)} %fusion.107), kind=kLoop, calls=%fused_computation.40 | loop fusion | flops 1792000 | bytes 515048 | tf_op jit(solution)/shard_map/convert.2
  101.3 1.3 pad_maximum_fusion
  102.6 0.5 convert_element_type.189
  103.4 104.5 %scatter_custom_fusion.1 = f32[1025]{0:T(1024)S(1)} fusion(s32[16384]{0:T(1024)S(1)} %bitcast.76, f32[16384]{0:T(1024)S(1)} %broadcast.429, f32[]{:T(128)} %constant.221.clone.1), kind=kCustom, calls=%fused_computation.127 | custom fusion | flops 16384 | bytes 4104 | tf_op jit(solution)/shard_map/scatter-add | solution.py:102
  207.8 244.0 %all-to-all-done.1 = bf16[250,64,256]{0,2,1:T(8,128)(2,1)} async-done(((bf16[250,64,256]{0,2,1:T(8,128)(2,1)}), bf16[250,64,256]{0,2,1:T(8,128)(2,1)}, u32[]{:S(2)}, u32[]{:S(2)}) %all-to-all-start.1) | async-done | bytes 8192032 | tf_op jit(solution)/shard_map/all_to_all | solution.py:84
  451.8 103.7 %scatter_custom_fusion.3 = f32[1025,250]{1,0:T(8,128)S(1)} fusion(s32[16384]{0:T(1024)S(1)} %bitcast.77, bf16[250,16384]{0,1:T(8,128)(2,1)} %bitcast.17, f32[]{:T(128)} %constant.221.clone.1), kind=kCustom, calls=%fused_computation.5 | custom fusion | flops 8192000 | bytes 9217004 | tf_op jit(solution)/shard_map/scatter-add | solution.py:101
  555.5 2.8 fusion.8
  558.3 34.0 %reduce-scatter.2.cloned.1.call-done = f32[64,2,1024]{2,0,1:T(8,128)} async-done(((f32[512,2,1024]{2,0,1:T(8,128)}), f32[64,2,1024]{2,0,1:T(8,128)}) %reduce-scatter.2.cloned.1.call-update) | async-done | bytes 524304 | tf_op jit(solution)/shard_map/reduce_scatter | solution.py:113
  592.4 2.2 copy.12
  594.6 15.5 %all-to-all-start.2 = ((f32[64,2,1024]{2,1,0:T(2,128)}), f32[64,2,1024]{2,1,0:T(2,128)S(1)}, u32[]{:S(2)}, u32[]{:S(2)}) async-start(f32[64,2,1024]{2,1,0:T(2,128)} %copy.12), calls=%async_computation.3 | async-start | bytes 1048576 | tf_op jit(solution)/shard_map/all_to_all | solution.py:119
  610.2 118.6 %all_gather.3 = bf16[65536]{0:T(1024)(128)(2,1)S(1)} all-gather(bf16[1024]{0:T(1024)(128)(2,1)S(1)} %minimum_convert_fusion), channel_id=1, replica_groups=mesh['bins'=64,'freq'=8] {'bins'}, dimensions={0}, use_global_device_ids=true | all-gather | bytes 133120 | tf_op jit(solution)/shard_map/all_gather | solution.py:120
  728.8 0.4 multiply_add_fusion
  729.2 1.4 slice_reduce_fusion.2
  730.7 1.6 fusion.60
  732.3 1.6 fusion.64
  733.9 1.6 convolution_subtract_fusion.7
  735.5 1.5 fusion.62
  737.0 1.6 fusion.23
  738.6 1.6 convolution_add_fusion.7
  740.2 2.0 convolution_subtract_fusion.6
  742.2 2.2 fusion.91
  745.0 1.6 fusion.53
  746.6 1.6 fusion.57
  748.2 1.6 convolution_subtract_fusion.5
  749.9 1.5 fusion.55
  751.4 1.6 fusion.78
  753.0 1.8 convolution_add_fusion.5
  754.8 1.6 fusion.2
  756.4 0.3 copy.14
  756.6 1.5 fusion.1
  758.2 0.3 copy.15
  758.5 0.8 fusion.7
  759.3 1.4 slice_reduce_fusion
  760.7 1.6 fusion.46
  762.4 1.6 fusion.50
  764.0 1.6 convolution_subtract_fusion.3
  765.5 1.8 fusion.48
  767.3 1.6 fusion.18
  768.9 1.6 convolution_add_fusion.3
  770.5 1.6 convolution_subtract_fusion.2
  772.1 2.2 fusion.87
  774.9 1.6 fusion.39
  776.5 1.6 fusion.43
  778.1 1.6 convolution_subtract_fusion.1
  779.8 1.8 fusion.41
  781.6 1.6 fusion.73
  783.1 1.6 convolution_add_fusion.1
  784.8 1.6 convolution_subtract_fusion
  786.3 0.3 stack.19
  786.6 1.6 convolution_add_fusion
  788.2 0.3 stack.20
  788.4 1.3 maximum_multiply_fusion.1
  (18 shorter events, 1.0 us)
Async XLA Ops:
  10.4 56.8 %all-to-all-start = ((s32[1,64,256]{2,0,1:T(1,128)}), s32[1,64,256]{2,0,1:T(1,128)S(1)}, u32[]{:S(2)}, u32[]{:S(2)}) async-start(s32[1,64,256]{2,0,1:T(1,128)} %bitcast.4), calls=%async_computation | async-start | bytes 131072 | tf_op jit(solution)/shard_map/all_to_all | solution.py:91
  67.3 384.5 %all-to-all-start.1 = ((bf16[250,64,256]{0,2,1:T(8,128)(2,1)}), bf16[250,64,256]{0,2,1:T(8,128)(2,1)}, u32[]{:S(2)}, u32[]{:S(2)}) async-start(bf16[250,64,256]{0,2,1:T(8,128)(2,1)} %bitcast.67), calls=%async_computation.1 | async-start | bytes 16777216 | tf_op jit(solution)/shard_map/all_to_all | solution.py:84
  82.6 509.8 %reduce-scatter.2.cloned.1.call-start = ((), (), s32[]{:S(2)}) async-start(), calls=%async_computation.4 | async-start | bytes 4718592 | tf_op jit(solution)/shard_map/reduce_scatter | solution.py:113
  594.6 134.2 %all-to-all-start.2 = ((f32[64,2,1024]{2,1,0:T(2,128)}), f32[64,2,1024]{2,1,0:T(2,128)S(1)}, u32[]{:S(2)}, u32[]{:S(2)}) async-start(f32[64,2,1024]{2,1,0:T(2,128)} %copy.12), calls=%async_computation.3 | async-start | bytes 1048576 | tf_op jit(solution)/shard_map/all_to_all | solution.py:119
Sparse Core Ops, SparseCore 0:
  558.4 33.8 reduce-scatter.1
where the time goes:
time: 804 us; the launch traced here: 797 us
  waiting for transfers between devices  278 us (35%)
  other arithmetic  234 us (29%)
  blocking collectives  119 us (15%)
  matrix products  55.5 us (7%)
  starting transfers between devices  49.8 us (6%)
  local copies, waits for them, and re-layouts  45.2 us (6%)
  between operations  15.6 us (2%)
    all_to_all x1, waiting for transfers between devices, local(): lax.all_to_all(data_buf.reshape(span, owners, capacity * tile_len), 'bins...  244 us
    all_gather x1, blocking collectives, local(): lax.all_gather(jnp.minimum(count, 1.0).astype(jnp.bfloat16), 'bins', axis...  119 us
    scatter-add x1, other arithmetic, local(): jax.ops.segment_sum(jnp.ones(flat_labels.shape, jnp.float32), flat_labels...  104 us
    scatter-add x1, other arithmetic, local(): jax.ops.segment_sum(columns, flat_labels, local_bins + 1)[:local_bins]  104 us
    dot_general x32, matrix products, exact_dot(): jnp.dot(left, right, precision=lax.Precision.HIGHEST, preferred_element_t...  52.7 us
    reduce_scatter x1, waiting for transfers between devices, local(): lax.psum_scatter(part.reshape(lax.axis_size('freq') * per_group, 2, local...  34 us
    scatter x2, local copies, waits for them, and re-layouts, local(): data_buf = jnp.zeros((span, owners * capacity, tile_len), jnp.bfloat16).a...  23.8 us
    all_to_all x1, starting transfers between devices, local(): lax.all_to_all(label_buf.reshape(1, owners, capacity * tile_len), 'bins',...  18.7 us
  transfers between devices with their start and end apart: 4, of which 2 were waited for; matrix products, arithmetic and copies ran while one was open for 20% of the time, Pallas kernels for 0%

commit v1 on v0

v1 whole, which is shorter than its diff:
```python
import functools
import math

import jax
import jax.numpy as jnp
import numpy as np
from jax import lax
from jax.experimental import pallas as pl
from jax.experimental.pallas import tpu as pltpu
from jax.sharding import PartitionSpec as P

MESH = pl.DeviceIdType.MESH
ITERS = 2
TILE = 128
LB = 1024
YN = 4
XN = 4
CN = 2
NQ = 8
BF_STEPS = 4
NJ = 4
F32 = jnp.float32
BF16 = jnp.bfloat16


def dft_table(zn, samples):
    groups = XN * CN
    total = samples * groups
    x, y, c, z = np.meshgrid(np.arange(XN), np.arange(YN), np.arange(CN), np.arange(zn), indexing="ij")
    freq = (((z * YN + y) * XN + x) * CN + c).reshape(-1)
    phase = ((freq[:, None] + 1) * np.arange(total)[None, :]) % total
    angle = phase.astype(np.float32) * np.float32(2.0 * math.pi / total)
    norm = np.float32(1.0 / math.sqrt(total))
    table = np.stack([np.cos(angle) * norm, -np.sin(angle) * norm], axis=1).astype(BF16)
    rows = table.reshape(2 * freq.size, groups, samples)
    return np.ascontiguousarray(rows.transpose(1, 0, 2))


def spectra_kernel(x_hbm, tab_hbm, lab_hbm, out_hbm, labs_hbm,
                   xm, tab, far_out, far_l, far_r, near_r_out, near_l_out, near_l, near_r, fin,
                   tab_sem, loc_sem, core_send, core_recv, far_send, far_recv, near_send, near_recv,
                   y_send, y_recv, lab_send, lab_recv, own_sem, lab_own):
    bins = lax.axis_index("bins")
    freq = lax.axis_index("freq")
    z, y = bins // YN, bins % YN
    x, c = freq // CN, freq % CN
    nq, chunk = xm.shape[1], xm.shape[3]
    half = nq * chunk
    blk = tab.shape[1] // XN
    part = blk // (YN * CN)
    right = (bins, lax.rem(x + 1, XN) * CN + c)
    left = (bins, lax.rem(x + XN - 1, XN) * CN + c)
    other = (bins, x * CN + (1 - c))

    def plane(dy, dc):
        return (z * YN + lax.rem(y + dy, YN), x * CN + lax.rem(c + dc, CN))

    peers = [(dy, dc) for dy in range(YN) for dc in range(CN) if (dy, dc) != (0, 0)]

    tab_copy = pltpu.make_async_copy(tab_hbm.at[pl.ds(x * CN, CN)], tab, tab_sem)
    tab_copy.start()

    def local_copy(q):
        return pltpu.make_async_copy(
            x_hbm.at[:, pl.ds(pl.multiple_of(c * half + q * chunk, chunk), chunk)], xm.at[c, q], loc_sem.at[q])

    def core_copy(q):
        return pltpu.make_async_remote_copy(
            src_ref=x_hbm.at[:, pl.ds(pl.multiple_of((1 - c) * half + q * chunk, chunk), chunk)], dst_ref=xm.at[c, q],
            send_sem=core_send.at[q], recv_sem=core_recv.at[q], device_id=other, device_id_type=MESH)

    def core_arrival(q):
        return pltpu.make_async_remote_copy(
            src_ref=x_hbm.at[:, pl.ds(pl.multiple_of(c * half + q * chunk, chunk), chunk)], dst_ref=xm.at[1 - c, q],
            send_sem=core_send.at[q], recv_sem=core_recv.at[q], device_id=other, device_id_type=MESH)

    @pl.loop(0, nq)
    def _(q):
        local_copy(q).start()

    barrier = pltpu.get_barrier_semaphore()
    for device in [left, right] + [plane(dy, dc) for dy, dc in peers]:
        pl.semaphore_signal(barrier, inc=1, device_id=device, device_id_type=MESH)
    pl.semaphore_wait(barrier, 2 + len(peers))

    @pl.loop(0, nq)
    def _(q):
        core_copy(q).start()

    def lab_copy(dy):
        return pltpu.make_async_remote_copy(
            src_ref=lab_hbm, dst_ref=labs_hbm.at[y], send_sem=lab_send.at[dy - 1], recv_sem=lab_recv.at[dy - 1],
            device_id=plane(dy, 0), device_id_type=MESH)

    lab_local = pltpu.make_async_copy(lab_hbm, labs_hbm.at[y], lab_own)
    lab_local.start()
    for dy in range(1, YN):
        lab_copy(dy).start()

    def product(dest, q):
        rows = pl.ds(pl.multiple_of(dest * blk, blk), blk)
        first = jnp.dot(tab[0, rows, :], xm[0, q], preferred_element_type=F32)
        return first + jnp.dot(tab[1, rows, :], xm[1, q], preferred_element_type=F32)

    def far_copy(q, side):
        target = right if side == 0 else left
        rows = pl.ds(side * (blk // 2), blk // 2)
        land = far_l if side == 0 else far_r
        return pltpu.make_async_remote_copy(
            src_ref=far_out.at[q, rows], dst_ref=land.at[q], send_sem=far_send.at[side, q],
            recv_sem=far_recv.at[side, q], device_id=target, device_id_type=MESH)

    def near_copy(q, side):
        target = right if side == 0 else left
        source = near_r_out if side == 0 else near_l_out
        land = near_l if side == 0 else near_r
        return pltpu.make_async_remote_copy(
            src_ref=source.at[q], dst_ref=land.at[q], send_sem=near_send.at[side, q],
            recv_sem=near_recv.at[side, q], device_id=target, device_id_type=MESH)

    def y_copy(q, i):
        dy, dc = peers[i]
        to_y, to_c = lax.rem(y + dy, YN), lax.rem(c + dc, CN)
        rows = pl.ds(pl.multiple_of((to_y * CN + to_c) * part, part), part)
        return pltpu.make_async_remote_copy(
            src_ref=fin.at[q, rows], dst_ref=out_hbm.at[y * CN + c, q], send_sem=y_send.at[i, q],
            recv_sem=y_recv.at[i, q], device_id=plane(dy, dc), device_id_type=MESH)

    def own_copy(q):
        rows = pl.ds(pl.multiple_of((y * CN + c) * part, part), part)
        return pltpu.make_async_copy(fin.at[q, rows], out_hbm.at[y * CN + c, q], own_sem.at[q])

    tab_copy.wait()

    @pl.loop(0, nq)
    def _(q):
        local_copy(q).wait()
        core_arrival(q).wait_recv()
        far_out[q] = product(lax.rem(x + 2, XN), q).astype(BF16)
        far_copy(q, 0).start()
        far_copy(q, 1).start()

    @pl.loop(0, nq)
    def _(q):
        to_right = product(lax.rem(x + 1, XN), q)
        to_left = product(lax.rem(x + XN - 1, XN), q)
        far_copy(q, 0).wait_recv()
        near_r_out[q, : blk // 2] = (to_right[: blk // 2] + far_l[q].astype(F32)).astype(BF16)
        near_r_out[q, blk // 2:] = to_right[blk // 2:].astype(BF16)
        near_copy(q, 0).start()
        far_copy(q, 1).wait_recv()
        near_l_out[q, : blk // 2] = to_left[: blk // 2].astype(BF16)
        near_l_out[q, blk // 2:] = (to_left[blk // 2:] + far_r[q].astype(F32)).astype(BF16)
        near_copy(q, 1).start()

    @pl.loop(0, nq)
    def _(q):
        mine = product(x, q)
        near_copy(q, 0).wait_recv()
        near_copy(q, 1).wait_recv()
        fin[q] = (mine + (near_l[q].astype(F32) + near_r[q].astype(F32))).astype(BF16)
        for i in range(len(peers)):
            y_copy(q, i).start()
        own_copy(q).start()

    @pl.loop(0, nq)
    def _(q):
        core_copy(q).wait_send()
        for side in (0, 1):
            far_copy(q, side).wait_send()
            near_copy(q, side).wait_send()
        for i in range(len(peers)):
            y_copy(q, i).wait()
        own_copy(q).wait()

    for dy in range(1, YN):
        lab_copy(dy).wait()
    lab_local.wait()


def spectra(traces, table, labels):
    samples, width = traces.shape
    groups, rows, _ = table.shape
    half = width // CN
    nq = min(NQ, half // 512)
    chunk = half // nq
    blk = rows // XN
    part = blk // (YN * CN)
    dma = pltpu.SemaphoreType.DMA
    npeer = YN * CN - 1
    any_spec = pl.BlockSpec(memory_space=pl.ANY)
    return pl.pallas_call(
        spectra_kernel,
        out_shape=(
            jax.ShapeDtypeStruct((YN * CN, nq, part, chunk), BF16),
            jax.ShapeDtypeStruct((YN,) + labels.shape, jnp.int32),
        ),
        in_specs=[any_spec] * 3,
        out_specs=(any_spec, any_spec),
        scratch_shapes=[
            pltpu.VMEM((CN, nq, samples, chunk), BF16),
            pltpu.VMEM((CN, rows, samples), BF16),
            pltpu.VMEM((nq, blk, chunk), BF16),
            pltpu.VMEM((nq, blk // 2, chunk), BF16),
            pltpu.VMEM((nq, blk // 2, chunk), BF16),
            pltpu.VMEM((nq, blk, chunk), BF16),
            pltpu.VMEM((nq, blk, chunk), BF16),
            pltpu.VMEM((nq, blk, chunk), BF16),
            pltpu.VMEM((nq, blk, chunk), BF16),
            pltpu.VMEM((nq, blk, chunk), BF16),
            dma, dma((nq,)), dma((nq,)), dma((nq,)), dma((2, nq)), dma((2, nq)), dma((2, nq)), dma((2, nq)),
            dma((npeer, nq)), dma((npeer, nq)), dma((YN - 1,)), dma((YN - 1,)), dma((nq,)), dma,
        ],
        compiler_params=pltpu.CompilerParams(
            collective_id=0, has_side_effects=True, vmem_limit_bytes=56 * 1024 * 1024),
        cost_estimate=pl.CostEstimate(flops=2 * rows * samples * width, bytes_accessed=12 << 20, transcendentals=0),
        name="spectra",
    )(traces, table, labels)


def bin_kernel(own_ref, val_ref, lab_ref, acc_ref, cnt_ref):
    step = pl.program_id(0)
    _, nq, part, chunk = val_ref.shape
    per = chunk // TILE

    @pl.when(step == 0)
    def _():
        acc_ref[...] = jnp.zeros_like(acc_ref)
        cnt_ref[...] = jnp.zeros_like(cnt_ref)

    high = lax.broadcasted_iota(jnp.int32, (LB // TILE, TILE), 0)
    low = lax.broadcasted_iota(jnp.int32, (TILE, TILE), 0)

    @pl.loop(0, nq)
    def _(q):
        for r in range(per):
            tile = step * (nq * per) + q * per + r
            label = lab_ref[pl.ds(q * per + r, 1), :] & 2047
            vals = val_ref[0, q, :, r * TILE:(r + 1) * TILE].astype(F32)
            hot_high = (label // TILE == high).astype(F32)
            hot_low = ((label & (TILE - 1)) == low).astype(F32).astype(BF16)
            spread = (vals[:, None, :] * hot_high[None]).reshape(part * (LB // TILE), TILE)
            left = jnp.concatenate([spread, hot_high], axis=0).astype(BF16)
            sums = lax.dot_general(left, hot_low, (((1,), (1,)), ((), ())), preferred_element_type=F32)
            rows = pl.ds(pl.multiple_of(own_ref[tile] * (LB // TILE), LB // TILE), LB // TILE)
            acc_ref[:, rows, :] += sums[: part * (LB // TILE)].reshape(part, LB // TILE, TILE)
            cnt_ref[rows, :] += sums[part * (LB // TILE):]


def bin_plane(owners, vals, labels, n_owners):
    src, nq, part, chunk = vals.shape
    tiles = labels.shape[0]
    rows = n_owners * (LB // TILE)
    return pl.pallas_call(
        bin_kernel,
        grid_spec=pltpu.PrefetchScalarGridSpec(
            num_scalar_prefetch=1,
            grid=(src,),
            in_specs=[
                pl.BlockSpec((1, nq, part, chunk), lambda i, own: (i, 0, 0, 0)),
                pl.BlockSpec((tiles // src, TILE), lambda i, own: (i, 0)),
            ],
            out_specs=[
                pl.BlockSpec((part, rows, TILE), lambda i, own: (0, 0, 0)),
                pl.BlockSpec((rows, TILE), lambda i, own: (0, 0)),
            ],
        ),
        out_shape=(
            jax.ShapeDtypeStruct((part, rows, TILE), F32),
            jax.ShapeDtypeStruct((rows, TILE), F32),
        ),
        compiler_params=pltpu.CompilerParams(vmem_limit_bytes=56 * 1024 * 1024),
        name="bin_plane",
    )(owners, vals, labels)


def reduce_kernel(zn, bf_steps, acc_hbm, cnt_hbm, out_ref, tot_ref,
                  own, rb, sb, rf, sf, cz,
                  own_sem, b_send, b_recv, f_send, f_recv, cz_own, cz_send, cz_recv, g_send, g_recv):
    bins = lax.axis_index("bins")
    freq = lax.axis_index("freq")
    z, y = bins // YN, bins % YN
    x, c = freq // CN, freq % CN
    hops = zn // 2
    nj = NJ
    crow = cz.shape[1]
    rows = own.shape[2]
    place = (y * XN + x) * CN + c

    def along_z(dz):
        return (lax.rem(z + dz, zn) * YN + y, freq)

    nexts = (along_z(1), along_z(zn - 1))
    x_peer = [(bins, lax.rem(x + dx, XN) * CN + c) for dx in range(1, XN)]
    y_peer = [(z * YN + lax.rem(y + dy, YN), freq) for dy in range(1, YN)]
    c_peer = (bins, x * CN + 1 - c)

    def dest_of(slot):
        if slot == 0:
            return lax.rem(z + hops, zn)
        if slot < hops:
            return lax.rem(z + hops - slot, zn)
        if slot < 2 * hops - 1:
            return lax.rem(z + hops + (slot - hops + 1), zn)
        return z

    order = [0]
    for s in range(1, hops):
        order += [s, hops - 1 + s]
    order += [2 * hops - 1]

    def own_copy(slot):
        return pltpu.make_async_copy(acc_hbm.at[pl.ds(dest_of(slot) * 2, 2)], own.at[slot], own_sem.at[slot])

    for slot in order:
        own_copy(slot).start()
    mine = pl.ds(pl.multiple_of(place * crow, crow), crow)
    cnt_own = pltpu.make_async_copy(cnt_hbm.at[mine], cz.at[z], cz_own)
    cnt_own.start()

    barrier = pltpu.get_barrier_semaphore()

    @pl.loop(1, zn)
    def _(dz):
        pl.semaphore_signal(barrier, inc=1, device_id=along_z(dz), device_id_type=MESH)

    for device in x_peer + y_peer + [c_peer]:
        pl.semaphore_signal(barrier, inc=1, device_id=device, device_id_type=MESH)
    pl.semaphore_wait(barrier, zn - 1 + len(x_peer) + len(y_peer) + 1)

    def cz_copy(dz):
        return pltpu.make_async_remote_copy(
            src_ref=cnt_hbm.at[mine], dst_ref=cz.at[z], send_sem=cz_send.at[dz - 1], recv_sem=cz_recv.at[dz - 1],
            device_id=along_z(dz), device_id_type=MESH)

    def b_copy(side, s, j):
        return pltpu.make_async_remote_copy(
            src_ref=sb.at[side, s, j], dst_ref=rb.at[side, s, j], send_sem=b_send.at[side, s, j],
            recv_sem=b_recv.at[side, s, j], device_id=nexts[side], device_id_type=MESH)

    def f_copy(side, s, j):
        return pltpu.make_async_remote_copy(
            src_ref=sf.at[side, s - bf_steps, j], dst_ref=rf.at[side, s - bf_steps, j],
            send_sem=f_send.at[side, s - bf_steps, j],
            recv_sem=f_recv.at[side, s - bf_steps, j], device_id=nexts[side], device_id_type=MESH)

    per = rows * 2 // nj

    def own_piece(slot, j):
        first = j * per // rows
        return own[slot, first, (j * per) % rows:(j * per) % rows + per, :]

    own_copy(0).wait()
    for j in range(nj):
        side = 0 if j < nj // 2 else 1
        sb[side, 0, j] = own_piece(0, j).astype(BF16)
        b_copy(side, 0, j).start()

    @pl.loop(1, zn)
    def _(dz):
        cz_copy(dz).start()

    for s in range(1, hops):
        for side in (0, 1):
            slot = s if side == 0 else hops - 1 + s
            own_copy(slot).wait()
        for j in range(nj):
            for side in (0, 1):
                slot = s if side == 0 else hops - 1 + s
                piece = own_piece(slot, j)
                if s - 1 >= bf_steps:
                    f_copy(side, s - 1, j).wait_recv()
                    piece = piece + rf[side, s - 1 - bf_steps, j]
                elif s - 1 > 0 or (side == 0) == (j < nj // 2):
                    b_copy(side, s - 1, j).wait_recv()
                    piece = piece + rb[side, s - 1, j].astype(F32)
                if s < bf_steps:
                    sb[side, s, j] = piece.astype(BF16)
                    b_copy(side, s, j).start()
                else:
                    sf[side, s - bf_steps, j] = piece
                    f_copy(side, s, j).start()
        if s == 1:
            @pl.loop(1, zn)
            def _(dz):
                cz_copy(dz).wait()
            cnt_own.wait()
            tot_ref[pl.ds(place, 1)] = jnp.sum(cz[...], axis=0)[None]

        def gather(i, size, device):
            first = place // size * size
            part = pl.ds(first, size)
            return pltpu.make_async_remote_copy(
                src_ref=tot_ref.at[part], dst_ref=tot_ref.at[part], send_sem=g_send.at[i], recv_sem=g_recv.at[i],
                device_id=device, device_id_type=MESH)

        stages = [
            [(0, 1, c_peer)],
            [(1 + i, CN, device) for i, device in enumerate(x_peer)],
            [(XN + i, CN * XN, device) for i, device in enumerate(y_peer)],
        ]
        first_stage = max(1, hops - 5)
        for n, stage in enumerate(stages):
            if s == min(hops - 1, first_stage + n):
                if n:
                    for args in stages[n - 1]:
                        gather(*args).wait()
                for args in stage:
                    gather(*args).start()
        if s == hops - 1:
            for args in stages[-1]:
                gather(*args).wait()

    last = 2 * hops - 1
    own_copy(last).wait()
    for j in range(nj):
        for side in (0, 1):
            if hops > bf_steps:
                f_copy(side, hops - 1, j).wait_recv()
            else:
                b_copy(side, hops - 1, j).wait_recv()
        if hops > bf_steps:
            arrived = rf[0, hops - 1 - bf_steps, j] + rf[1, hops - 1 - bf_steps, j]
        else:
            arrived = rb[0, hops - 1, j].astype(F32) + rb[1, hops - 1, j].astype(F32)
        first = j * per // rows
        out_ref[first, (j * per) % rows:(j * per) % rows + per, :] = arrived + own_piece(last, j)

    for s in range(hops):
        for j in range(nj):
            for side in (0, 1):
                if s == 0 and (side == 0) != (j < nj // 2):
                    continue
                if s < bf_steps:
                    b_copy(side, s, j).wait_send()
                else:
                    f_copy(side, s, j).wait_send()


def reduce_planes(acc, cnt, zn):
    part, rows, _ = acc.shape
    hops = zn // 2
    bf = min(BF_STEPS, hops)
    fs = max(hops - bf, 1)
    per = rows * 2 // NJ
    places = YN * XN * CN
    crow = rows // places
    dma = pltpu.SemaphoreType.DMA
    any_spec = pl.BlockSpec(memory_space=pl.ANY)
    return pl.pallas_call(
        functools.partial(reduce_kernel, zn, bf),
        out_shape=(
            jax.ShapeDtypeStruct((2, rows, TILE), F32),
            jax.ShapeDtypeStruct((places, crow, TILE), F32),
        ),
        in_specs=[any_spec, any_spec],
        out_specs=(pl.BlockSpec(memory_space=pltpu.VMEM), pl.BlockSpec(memory_space=pltpu.VMEM)),
        scratch_shapes=[
            pltpu.VMEM((zn, 2, rows, TILE), F32),
            pltpu.VMEM((2, bf, NJ, per, TILE), BF16),
            pltpu.VMEM((2, bf, NJ, per, TILE), BF16),
            pltpu.VMEM((2, fs, NJ, per, TILE), F32),
            pltpu.VMEM((2, fs, NJ, per, TILE), F32),
            pltpu.VMEM((zn, crow, TILE), F32),
            dma((zn,)), dma((2, bf, NJ)), dma((2, bf, NJ)), dma((2, fs, NJ)), dma((2, fs, NJ)),
            dma, dma((zn - 1,)), dma((zn - 1,)), dma((7,)), dma((7,)),
        ],
        compiler_params=pltpu.CompilerParams(
            collective_id=1, has_side_effects=True, vmem_limit_bytes=56 * 1024 * 1024),
        cost_estimate=pl.CostEstimate(flops=0, bytes_accessed=12 << 20, transcendentals=0),
        name="reduce_planes",
    )(acc, cnt)


def grid_tables():
    index = np.arange(256)
    a, b = index // 16, index % 16
    phase = (a[:, None] * a[None, :] + b[:, None] * b[None, :]) % 16
    angle = 2.0 * np.pi * phase / 16.0
    cos, sin = np.cos(angle), np.sin(angle)
    forward = np.block([[cos, sin], [-sin, cos]]).astype(np.float32)
    inverse = np.block([[cos, -sin], [sin, cos]]).astype(np.float32)
    both = []
    for m in (forward, inverse):
        hi = m.astype(BF16)
        lo = (m - hi.astype(np.float32)).astype(BF16)
        both.append(np.stack([hi, lo]))
    return np.stack(both)


def split(value):
    hi = value.astype(BF16)
    return hi, (value - hi.astype(F32)).astype(BF16)


def mwni_kernel(sum_ref, cnt_ref, tab_ref, out_ref):
    n = 256

    def grid(ref):
        return jnp.concatenate([ref[pl.ds(0, n, stride=2), :], ref[pl.ds(1, n, stride=2), :]], axis=1)

    def left_dot(m, value):
        hi, lo = split(value)
        t_hi, t_lo = tab_ref[m, 0], tab_ref[m, 1]
        dot = functools.partial(jnp.dot, preferred_element_type=F32)
        return dot(t_hi, hi) + (dot(t_hi, lo) + dot(t_lo, hi))

    def right_dot(m, value):
        hi, lo = split(value)
        t_hi, t_lo = tab_ref[m, 0], tab_ref[m, 1]
        dot = functools.partial(jnp.dot, preferred_element_type=F32)
        return dot(hi, t_hi) + (dot(lo, t_hi) + dot(hi, t_lo))

    def transform(forward, re, im):
        mid = left_dot(0 if forward else 1, jnp.concatenate([re, im], axis=0))
        out = right_dot(1 if forward else 0, jnp.concatenate([mid[:n], mid[n:]], axis=1))
        return out[:, :n], out[:, n:]

    count = grid(cnt_ref)
    cover = jnp.minimum(count, 1.0)
    scale = 1.0 / jnp.maximum(count, 1.0)
    obs_re = grid(sum_ref.at[0]) * scale
    obs_im = grid(sum_ref.at[1]) * scale
    re, im = obs_re, obs_im
    cells = n * n
    for step in range(ITERS):
        u_re = cover * obs_re + (1.0 - cover) * re
        u_im = cover * obs_im + (1.0 - cover) * im
        f_re, f_im = transform(True, u_re, u_im)
        power = f_re * f_re + f_im * f_im
        lam = 0.5 * (jnp.sum(power) / cells) + 1e-06
        keep = power / (power + lam)
        re, im = transform(False, f_re * keep, f_im * keep)
        re, im = re * (1.0 / cells), im * (1.0 / cells)
    out_ref[0] = re
    out_ref[1] = im


def mwni(sums, counts, tables):
    vmem = pl.BlockSpec(memory_space=pltpu.VMEM)
    return pl.pallas_call(
        mwni_kernel,
        out_shape=jax.ShapeDtypeStruct((2, 256, 256), F32),
        in_specs=[vmem] * 3,
        out_specs=vmem,
        compiler_params=pltpu.CompilerParams(vmem_limit_bytes=56 * 1024 * 1024),
        name="mwni",
    )(sums, counts, tables)


def local(zn, table, tables, traces, bin_ids, valid, tile_owner):
    n_owners = zn * YN
    tiles = tile_owner.shape[0]
    labels = jnp.where(valid > 0, bin_ids, LB).reshape(tiles, TILE) + tile_owner * 2048
    vals, labs = spectra(traces, table, labels)
    labs = labs.reshape(YN * tiles, TILE)
    owners = labs[:, 0] // 2048
    acc, cnt = bin_plane(owners, vals, labs, n_owners)
    sums, counts = reduce_planes(acc, cnt, zn)
    state = mwni(sums, counts.reshape(-1, TILE), tables)
    return state.reshape(1, 2, -1)


def solution(mesh):
    zn = mesh.shape["bins"] // YN
    table = dft_table(zn, 250)
    tables = grid_tables()
    in_specs = (P("freq", "bins"), P("bins"), P("bins"), P("bins", None))
    out_specs = P(("bins", "freq"), None, None)

    def run(traces, bin_ids, valid, tile_owner):
        return jax.shard_map(
            functools.partial(local, zn, jnp.asarray(table), jnp.asarray(tables)),
            mesh=mesh, in_specs=in_specs, out_specs=out_specs, check_vma=False,
        )(traces, bin_ids, valid, tile_owner)

    return run
```

time: 804 us -> 218 us (0.27)
  waiting for transfers between devices: 278 us -> 0 us
  other arithmetic: 234 us -> 2.66 us
  Pallas kernels: 0 us -> 210 us
  blocking collectives: 119 us -> 0 us
  matrix products: 55.5 us -> 0 us
  starting transfers between devices: 49.8 us -> 0 us
  local copies, waits for them, and re-layouts: 45.2 us -> 3.19 us
  between operations: 15.6 us -> 0.02 us
    all_to_all x3 -> x0, waiting for transfers between devices: 244 us -> none  [the longest x1 244 us: local(): lax.all_to_all(data_buf.reshape(span, owners, capacity * tile_len), 'bins...]
    pallas_call x0 -> x4, Pallas kernels: none -> 210 us  [the longest x1 86.3 us: reduce_planes(): pl.pallas_call(functools.partial(reduce_kernel, zn, bf), out_shape=(jax.S...]
    scatter-add x2 -> x0, other arithmetic: 208 us -> none  [the longest x1 104 us: local(): jax.ops.segment_sum(jnp.ones(flat_labels.shape, jnp.float32), flat_labels...]
    all_gather x1 -> x0, blocking collectives: 119 us -> none  [local(): lax.all_gather(jnp.minimum(count, 1.0).astype(jnp.bfloat16), 'bins', axis...]
    dot_general x33 -> x0, matrix products: 55.5 us -> none  [the longest x32 52.7 us: exact_dot(): jnp.dot(left, right, precision=lax.Precision.HIGHEST, preferred_element_t...]
    all_to_all x3 -> x0, starting transfers between devices: 49.6 us -> none  [the longest x1 18.7 us: local(): lax.all_to_all(label_buf.reshape(1, owners, capacity * tile_len), 'bins',...]
    reduce_scatter x1 -> x0, waiting for transfers between devices: 34 us -> none  [local(): lax.psum_scatter(part.reshape(lax.axis_size('freq') * per_group, 2, local...]
    scatter x2 -> x0, local copies, waits for them, and re-layouts: 23.8 us -> none  [local(): data_buf = jnp.zeros((span, owners * capacity, tile_len), jnp.bfloat16).a...]
  transfers between devices with their start and end apart: 4 -> 0, of which waited for: 2 -> 0; matrix products, arithmetic and copies ran while one was open for 20% -> 0% of each run, Pallas kernels for 0% -> 0%
where the time goes in v1:
time: 218 us; the launch traced here: 216 us
  Pallas kernels  210 us (96%)
  local copies, waits for them, and re-layouts  3.19 us (1%)
  other arithmetic  2.66 us (1%)
    pallas_call x1, Pallas kernels, reduce_planes(): pl.pallas_call(functools.partial(reduce_kernel, zn, bf), out_shape=(jax.S...  86.3 us
    pallas_call x1, Pallas kernels, spectra(): pl.pallas_call(spectra_kernel, out_shape=(jax.ShapeDtypeStruct((YN * CN,...  85.8 us
    pallas_call x1, Pallas kernels, bin_plane(): pl.pallas_call(bin_kernel, grid_spec=pltpu.PrefetchScalarGridSpec(num_sca...  28.3 us
    pallas_call x1, Pallas kernels, mwni(): pl.pallas_call(mwni_kernel, out_shape=jax.ShapeDtypeStruct((2, 256, 256),...  9.9 us

profile of v1, /device:TPU:6, one launch (start us, length us, event | category | flops | bytes accessed | tf_op | source)
XLA Modules:
  0.0 216.1 jit_solution(17427175473413379776)
XLA Ops:
  0.0 0.7 multiply_bitcast_fusion
  0.7 1.5 bitcast_add_fusion.lab_hbm
  2.1 85.8 %spectra.1 = (bf16[8,8,32,512]{3,2,1,0:T(8,128)(2,1)}, s32[4,64,128]{2,1,0:T(8,128)}) custom-call(bf16[250,8192]{1,0:T(8,128)(2,1)} %x_hbm.1, bf16[8,1024,250]{2,1,0:T(8,128)(2,1)} %constant.25.clone.tab_hbm, s32[64,128]{1,0:T(8,128)} %bitcast_add_fusion.lab_hbm), custom_call_target="tpu_custom_call" | custom-call | flops 4194304000 | bytes 12582912 | tf_op jit(solution)/shard_map/spectra/pallas_call | solution.py:192
  87.9 1.0 slice_reduce_fusion
  88.9 0.5 and_select_fusion.own_ref
  89.4 28.3 %bin_plane.1 = (f32[32,512,128]{2,1,0:T(8,128)}, f32[512,128]{1,0:T(8,128)}) custom-call(s32[256]{0:T(256)} %and_select_fusion.own_ref, bf16[8,8,32,512]{3,2,1,0:T(8,128)(2,1)} %get-tuple-element.12.val_ref, s32[256,128]{1,0:T(8,128)} %bitcast.7), custom_call_target="tpu_custom_call" | custom-call | tf_op jit(solution)/shard_map/bin_plane/pallas_call | solution.py:254
  117.7 86.3 %reduce_planes.1 = (f32[2,512,128]{2,1,0:T(8,128)}, f32[32,16,128]{2,1,0:T(8,128)}) custom-call(f32[32,512,128]{2,1,0:T(8,128)} %get-tuple-element.13.acc_hbm, f32[512,128]{1,0:T(8,128)} %get-tuple-element.14.cnt_hbm), custom_call_target="tpu_custom_call" | custom-call | bytes 12582912 | tf_op jit(solution)/shard_map/reduce_planes/pallas_call | solution.py:450
  204.0 9.9 %mwni.1 = f32[2,256,256]{2,1,0:T(8,128)} custom-call(f32[2,512,128]{2,1,0:T(8,128)} %get-tuple-element.15.sum_ref, f32[512,128]{1,0:T(8,128)} %bitcast.8, bf16[2,2,512,512]{3,2,1,0:T(8,128)(2,1)} %constant.26.clone.tab_ref), custom_call_target="tpu_custom_call" | custom-call | tf_op jit(solution)/shard_map/mwni/pallas_call | solution.py:541
  213.9 2.2 %reshape.15 = f32[1,2,65536]{2,1,0:T(2,128)} reshape(f32[2,256,256]{2,1,0:T(8,128)} %mwni.1) | data formatting | bytes 1048576 | tf_op jit(solution)/shard_map/reshape | solution.py:561

commit v2 on v0

v2 whole, which is shorter than its diff:
```python
import functools
import math

import jax
import jax.numpy as jnp
import numpy as np
from jax import lax
from jax.experimental import pallas as pl
from jax.experimental.pallas import tpu as pltpu
from jax.sharding import PartitionSpec as P

MESH = pl.DeviceIdType.MESH
ITERS = 2
TILE = 128
LB = 1024
YN = 4
XN = 4
CN = 2
NQ = 8
BF_STEPS = 6
NJ = 4
F32 = jnp.float32
BF16 = jnp.bfloat16


def dft_table(zn, samples):
    groups = XN * CN
    total = samples * groups
    x, y, c, z = np.meshgrid(np.arange(XN), np.arange(YN), np.arange(CN), np.arange(zn), indexing="ij")
    freq = (((z * YN + y) * XN + x) * CN + c).reshape(-1)
    phase = ((freq[:, None] + 1) * np.arange(total)[None, :]) % total
    angle = phase.astype(np.float32) * np.float32(2.0 * math.pi / total)
    norm = np.float32(1.0 / math.sqrt(total))
    table = np.stack([np.cos(angle) * norm, -np.sin(angle) * norm], axis=0).astype(BF16)
    rows = table.reshape(2 * freq.size, groups, samples)
    return np.ascontiguousarray(rows.transpose(1, 0, 2))


HIGH = LB // TILE


def observe_kernel(zn, x_hbm, tab_hbm, ids_ref, valid_ref, owner_ref, out_ref, tot_ref,
                   xm, tab, far_out, far_l, far_r, near_r_out, near_l_out, near_l, near_r, fin,
                   plane0, plane1, acc0, acc1, cnt, pay, labs, slots, rb, sb, rf, sf, cz,
                   tab_sem, loc_sem, core_send, core_recv, far_send, far_recv, near_send, near_recv,
                   y_send, y_recv, own_sem, lab_send, lab_recv, lab_own, slot_sem,
                   b_send, b_recv, f_send, f_recv, cz_own, cz_send, cz_recv, g_send, g_recv):
    bins = lax.axis_index("bins")
    freq = lax.axis_index("freq")
    z, y = bins // YN, bins % YN
    x, c = freq // CN, freq % CN
    nq, chunk = xm.shape[1], xm.shape[3]
    per_chunk = chunk // TILE
    half = nq * chunk
    blk = tab.shape[1] // XN // 2
    part = blk // (YN * CN)
    tiles = ids_ref.shape[0]
    hops = zn // 2
    rows = acc0.shape[1]
    nj = NJ
    per = rows // nj
    crow = cz.shape[1]
    place = (y * XN + x) * CN + c
    spectra, accs = (plane0, plane1), (acc0, acc1)

    right = (bins, lax.rem(x + 1, XN) * CN + c)
    left = (bins, lax.rem(x + XN - 1, XN) * CN + c)
    other = (bins, x * CN + (1 - c))

    def plane(dy, dc):
        return (z * YN + lax.rem(y + dy, YN), x * CN + lax.rem(c + dc, CN))

    def along_z(dz):
        return (lax.rem(z + dz, zn) * YN + y, freq)

    nexts = (along_z(1), along_z(zn - 1))
    peers = [(dy, dc) for dy in range(YN) for dc in range(CN) if (dy, dc) != (0, 0)]
    x_peer = [(bins, lax.rem(x + dx, XN) * CN + c) for dx in range(1, XN)]
    y_peer = [plane(dy, 0) for dy in range(1, YN)]

    def remote(src, dst, send, recv, device):
        return pltpu.make_async_remote_copy(
            src_ref=src, dst_ref=dst, send_sem=send, recv_sem=recv, device_id=device, device_id_type=MESH)

    tab_copy = pltpu.make_async_copy(tab_hbm.at[pl.ds(x * CN, CN)], tab, tab_sem)
    tab_copy.start()

    def piece_of(side, q):
        return x_hbm.at[:, pl.ds(pl.multiple_of(side * half + q * chunk, chunk), chunk)]

    def local_copy(q):
        return pltpu.make_async_copy(piece_of(c, q), xm.at[c, q], loc_sem.at[q])

    def core_copy(q):
        return remote(piece_of(1 - c, q), xm.at[c, q], core_send.at[q], core_recv.at[q], other)

    def core_arrival(q):
        return remote(piece_of(c, q), xm.at[1 - c, q], core_send.at[q], core_recv.at[q], other)

    @pl.loop(0, nq)
    def _(q):
        local_copy(q).start()

    barrier = pltpu.get_barrier_semaphore()
    for device in [left, right] + [plane(dy, dc) for dy, dc in peers]:
        pl.semaphore_signal(barrier, inc=1, device_id=device, device_id_type=MESH)
    pl.semaphore_signal(barrier, inc=1, device_id=x_peer[1], device_id_type=MESH)

    @pl.loop(1, zn)
    def _(dz):
        pl.semaphore_signal(barrier, inc=1, device_id=along_z(dz), device_id_type=MESH)

    pay[:tiles] = jnp.where(valid_ref[...] > 0, ids_ref[...], LB)
    tile_no = lax.broadcasted_iota(jnp.int32, (tiles, TILE), 0)
    named = owner_ref[...] == lax.broadcasted_iota(jnp.int32, (tiles, TILE), 1)
    none = tiles + 2
    first = jnp.min(jnp.where(named, tile_no, none), axis=0, keepdims=True)
    second = jnp.max(jnp.where(named, tile_no, -1), axis=0, keepdims=True)
    second = jnp.where(second > first, second, none)
    tail_row = lax.broadcasted_iota(jnp.int32, (8, TILE), 0)
    pay[tiles:tiles + 8] = jnp.where(tail_row == 0, first, jnp.where(tail_row == 1, second, LB))

    pl.semaphore_wait(barrier, 3 + len(peers) + zn - 1)

    @pl.loop(0, nq)
    def _(q):
        core_copy(q).start()

    def lab_copy(dy):
        return remote(pay, labs.at[y], lab_send.at[dy - 1], lab_recv.at[dy - 1], plane(dy, 0))

    lab_local = pltpu.make_async_copy(pay, labs.at[y], lab_own)
    lab_local.start()
    for dy in range(1, YN):
        lab_copy(dy).start()

    def product(h, dest, q):
        block = pl.ds(pl.multiple_of(h * (blk * XN) + dest * blk, blk), blk)
        return (jnp.dot(tab[0, block, :], xm[0, q], preferred_element_type=F32)
                + jnp.dot(tab[1, block, :], xm[1, q], preferred_element_type=F32))

    def far_copy(hq, side):
        target, land = ((right, far_l), (left, far_r))[side]
        return remote(far_out.at[hq, pl.ds(side * (blk // 2), blk // 2)], land.at[hq],
                      far_send.at[side, hq], far_recv.at[side, hq], target)

    def near_copy(hq, side):
        target, source, land = ((right, near_r_out, near_l), (left, near_l_out, near_r))[side]
        return remote(source.at[hq], land.at[hq], near_send.at[side, hq], near_recv.at[side, hq], target)

    def y_copy(h, q, i):
        dy, dc = peers[i]
        block = pl.ds(pl.multiple_of((lax.rem(y + dy, YN) * CN + lax.rem(c + dc, CN)) * part, part), part)
        return remote(fin.at[h * nq + q, :, block], spectra[h].at[(y * CN + c) * nq + q],
                      y_send.at[h, i, q], y_recv.at[h, i, q], plane(dy, dc))

    def own_copy(h, q):
        block = pl.ds(pl.multiple_of((y * CN + c) * part, part), part)
        return pltpu.make_async_copy(
            fin.at[h * nq + q, :, block], spectra[h].at[(y * CN + c) * nq + q], own_sem.at[h, q])

    def far_step(h, q):
        hq = h * nq + q
        far_out[hq] = product(h, lax.rem(x + 2, XN), q).astype(BF16)
        far_copy(hq, 0).start()
        far_copy(hq, 1).start()

    def near_step(h, q):
        hq = h * nq + q
        to_right = product(h, lax.rem(x + 1, XN), q)
        to_left = product(h, lax.rem(x + XN - 1, XN), q)
        mid = blk // 2
        far_copy(hq, 0).wait_recv()
        near_r_out[hq, :mid] = (to_right[:mid] + far_l[hq].astype(F32)).astype(BF16)
        near_r_out[hq, mid:] = to_right[mid:].astype(BF16)
        near_copy(hq, 0).start()
        far_copy(hq, 1).wait_recv()
        near_l_out[hq, :mid] = to_left[:mid].astype(BF16)
        near_l_out[hq, mid:] = (to_left[mid:] + far_r[hq].astype(F32)).astype(BF16)
        near_copy(hq, 1).start()

    def final_step(h, q):
        hq = h * nq + q
        mine = product(h, x, q)
        near_copy(hq, 0).wait_recv()
        near_copy(hq, 1).wait_recv()
        full = (mine + (near_l[hq].astype(F32) + near_r[hq].astype(F32))).astype(BF16)
        for r in range(per_chunk):
            fin[hq, r] = full[:, r * TILE:(r + 1) * TILE]
        for i in range(len(peers)):
            y_copy(h, q, i).start()
        own_copy(h, q).start()

    low_iota = [(lax.broadcasted_iota(jnp.int32, (16, TILE), 0) + 16 * i).astype(F32).astype(BF16)
                for i in range(TILE // 16)]
    one, zero = jnp.ones((16, TILE), BF16), jnp.zeros((16, TILE), BF16)

    def bin_owner(h, o):
        lefts, rights = [], []
        for yy in range(YN):
            for rank in range(2):
                t = slots[yy, rank, o]
                label = labs[yy, pl.ds(t, 1), :]
                tv = jnp.minimum(t, tiles - 1)
                vals = spectra[h][yy * (tiles // per_chunk) + tv // per_chunk, tv % per_chunk]
                low = jnp.broadcast_to((label & (TILE - 1)).astype(F32), (16, TILE)).astype(BF16)
                high = jnp.broadcast_to((label // TILE).astype(F32), (16, TILE)).astype(BF16)
                pieces = [jnp.where(high == jnp.asarray(k, BF16), vals, zero) for k in range(HIGH)]
                if h == 0:
                    pieces.append(jnp.where(high == low_iota[0], one, zero))
                lefts.append(jnp.concatenate(pieces, axis=0))
                rights.append(jnp.concatenate([jnp.where(low == it, one, zero) for it in low_iota], axis=0))
        sums = lax.dot_general(jnp.concatenate(lefts, axis=1), jnp.concatenate(rights, axis=1),
                               (((1,), (1,)), ((), ())), preferred_element_type=F32)
        where = pl.ds(pl.multiple_of(o * HIGH, HIGH), HIGH)
        accs[h][:, where, :] = jnp.swapaxes(sums[: HIGH * part].reshape(HIGH, part, TILE), 0, 1)
        if h == 0:
            cnt[where, :] = sums[HIGH * part: HIGH * part + HIGH]

    def bin_range(h, j):
        owners = per // HIGH

        @pl.loop(j * owners, (j + 1) * owners)
        def _(o):
            bin_owner(h, o)

    def b_copy(h, side, s, j):
        return remote(sb.at[h, side, s, j], rb.at[h, side, s, j],
                      b_send.at[h, side, s, j], b_recv.at[h, side, s, j], nexts[side])

    def f_copy(h, side, s, j):
        k = s - BF_STEPS
        return remote(sf.at[h, side, k, j], rf.at[h, side, k, j],
                      f_send.at[h, side, k, j], f_recv.at[h, side, k, j], nexts[side])

    def z_send(h, side, s, j, value):
        if s < BF_STEPS:
            sb[h, side, s, j] = value.astype(BF16)
            b_copy(h, side, s, j).start()
        else:
            sf[h, side, s - BF_STEPS, j] = value
            f_copy(h, side, s, j).start()

    def z_take(h, side, s, j):
        if s < BF_STEPS:
            b_copy(h, side, s, j).wait_recv()
            return rb[h, side, s, j].astype(F32)
        f_copy(h, side, s, j).wait_recv()
        return rf[h, side, s - BF_STEPS, j]

    def first_side(j):
        return 0 if j < nj // 2 else 1

    def z_item(h, s, j):
        span = slice(j * per, (j + 1) * per)
        if s == 0:
            bin_range(h, j)
            z_send(h, first_side(j), 0, j, accs[h][lax.rem(z + hops, zn), span, :])
        elif s < hops:
            for side in (0, 1):
                dest = lax.rem(z + hops - s, zn) if side == 0 else lax.rem(z + zn - hops + s, zn)
                value = accs[h][dest, span, :]
                if s > 1 or side == first_side(j):
                    value = value + z_take(h, side, s - 1, j)
                z_send(h, side, s, j, value)
        else:
            value = z_take(h, 0, hops - 1, j) + z_take(h, 1, hops - 1, j)
            out_ref[h, span, :] = value + accs[h][z, span, :]

    mine_rows = pl.ds(pl.multiple_of(place * crow, crow), crow)

    def cz_copy(dz):
        return remote(cnt.at[mine_rows], cz.at[z], cz_send.at[dz - 1], cz_recv.at[dz - 1], along_z(dz))

    cnt_own = pltpu.make_async_copy(cnt.at[mine_rows], cz.at[z], cz_own)

    def gather(i, size, device):
        part_of = pl.ds(place // size * size, size)
        return remote(tot_ref.at[part_of], tot_ref.at[part_of], g_send.at[i], g_recv.at[i], device)

    stages = [
        [(0, 1, other)],
        [(1 + i, CN, device) for i, device in enumerate(x_peer)],
        [(XN + i, CN * XN, device) for i, device in enumerate(y_peer)],
    ]

    tab_copy.wait()

    @pl.loop(0, nq)
    def _(q):
        local_copy(q).wait()
        core_arrival(q).wait_recv()
        far_step(0, q)

    @pl.loop(0, nq)
    def _(q):
        near_step(0, q)

    @pl.loop(0, nq)
    def _(q):
        final_step(0, q)
        far_step(1, q)

    for dy in range(1, YN):
        lab_copy(dy).wait()
    lab_local.wait()
    slot_copy = pltpu.make_async_copy(labs.at[:, pl.ds(tiles, 8)], slots, slot_sem)
    slot_copy.start()
    slot_copy.wait()

    def plane_arrived(h):
        @pl.loop(0, nq)
        def _(q):
            for i in range(len(peers)):
                y_copy(h, q, i).wait_recv()
            own_copy(h, q).wait()

    plane_arrived(0)
    lag = hops
    pair = max(1, nq // 4)
    near_at, final_at = 2, 5
    for d in range(lag + hops + nj):
        for j in range(nj):
            if 0 <= d - j <= hops:
                z_item(0, d - j, j)
        if near_at <= d < near_at + nq // pair:
            @pl.loop((d - near_at) * pair, (d - near_at + 1) * pair)
            def _(q):
                near_step(1, q)
        if final_at <= d < final_at + nq // pair:
            @pl.loop((d - final_at) * pair, (d - final_at + 1) * pair)
            def _(q):
                final_step(1, q)
        if d == lag:
            plane_arrived(1)
        for j in range(nj):
            if 0 <= d - lag - j <= hops:
                z_item(1, d - lag - j, j)
        if d == nj:
            cnt_own.start()

            @pl.loop(1, zn)
            def _(dz):
                cz_copy(dz).start()
        if d == nj + 3:
            @pl.loop(1, zn)
            def _(dz):
                cz_copy(dz).wait()
            cnt_own.wait()
            tot_ref[pl.ds(place, 1)] = jnp.sum(cz[...], axis=0)[None]
            for args in stages[0]:
                gather(*args).start()
        if d == nj + 5:
            for args in stages[0]:
                gather(*args).wait()
            for args in stages[1]:
                gather(*args).start()
        if d == nj + 7:
            for args in stages[1]:
                gather(*args).wait()
            for args in stages[2]:
                gather(*args).start()

    for args in stages[2]:
        gather(*args).wait()

    @pl.loop(0, nq)
    def _(q):
        core_copy(q).wait_send()
        for h in (0, 1):
            for side in (0, 1):
                far_copy(h * nq + q, side).wait_send()
                near_copy(h * nq + q, side).wait_send()
            for i in range(len(peers)):
                y_copy(h, q, i).wait_send()

    for h in (0, 1):
        for s in range(hops):
            for j in range(nj):
                for side in (0, 1):
                    if s == 0 and side != first_side(j):
                        continue
                    if s < BF_STEPS:
                        b_copy(h, side, s, j).wait_send()
                    else:
                        f_copy(h, side, s, j).wait_send()


def observe(zn, traces, table, ids, valid, owner):
    samples, width = traces.shape
    _, table_rows, _ = table.shape
    half = width // CN
    nq = NQ
    chunk = half // nq
    blk = table_rows // XN // 2
    part = blk // (YN * CN)
    tiles = ids.shape[0]
    hops = zn // 2
    fs = hops - BF_STEPS
    rows = zn * YN * HIGH
    per = rows // NJ
    places = YN * XN * CN
    crow = rows // places
    npeer = YN * CN - 1
    dma = pltpu.SemaphoreType.DMA
    any_spec = pl.BlockSpec(memory_space=pl.ANY)
    vmem = pl.BlockSpec(memory_space=pltpu.VMEM)
    plane_buf = pltpu.VMEM((YN * CN * nq, chunk // TILE, part, TILE), BF16)
    return pl.pallas_call(
        functools.partial(observe_kernel, zn),
        out_shape=(
            jax.ShapeDtypeStruct((2, rows, TILE), F32),
            jax.ShapeDtypeStruct((places, crow, TILE), F32),
        ),
        in_specs=[any_spec, any_spec, vmem, vmem, vmem],
        out_specs=(vmem, vmem),
        scratch_shapes=[
            pltpu.VMEM((CN, nq, samples, chunk), BF16),
            pltpu.VMEM((CN, table_rows, samples), BF16),
            pltpu.VMEM((2 * nq, blk, chunk), BF16),
            pltpu.VMEM((2 * nq, blk // 2, chunk), BF16),
            pltpu.VMEM((2 * nq, blk // 2, chunk), BF16),
            pltpu.VMEM((2 * nq, blk, chunk), BF16),
            pltpu.VMEM((2 * nq, blk, chunk), BF16),
            pltpu.VMEM((2 * nq, blk, chunk), BF16),
            pltpu.VMEM((2 * nq, blk, chunk), BF16),
            pltpu.VMEM((2 * nq, chunk // TILE, blk, TILE), BF16),
            plane_buf, plane_buf,
            pltpu.VMEM((part, rows, TILE), F32),
            pltpu.VMEM((part, rows, TILE), F32),
            pltpu.VMEM((rows, TILE), F32),
            pltpu.VMEM((tiles + 8, TILE), jnp.int32),
            pltpu.VMEM((YN, tiles + 8, TILE), jnp.int32),
            pltpu.SMEM((YN, 8, TILE), jnp.int32),
            pltpu.VMEM((2, 2, BF_STEPS, NJ, per, TILE), BF16),
            pltpu.VMEM((2, 2, BF_STEPS, NJ, per, TILE), BF16),
            pltpu.VMEM((2, 2, fs, NJ, per, TILE), F32),
            pltpu.VMEM((2, 2, fs, NJ, per, TILE), F32),
            pltpu.VMEM((zn, crow, TILE), F32),
            dma, dma((nq,)), dma((nq,)), dma((nq,)),
            dma((2, 2 * nq)), dma((2, 2 * nq)), dma((2, 2 * nq)), dma((2, 2 * nq)),
            dma((2, npeer, nq)), dma((2, npeer, nq)), dma((2, nq)),
            dma((YN - 1,)), dma((YN - 1,)), dma, dma,
            dma((2, 2, BF_STEPS, NJ)), dma((2, 2, BF_STEPS, NJ)), dma((2, 2, fs, NJ)), dma((2, 2, fs, NJ)),
            dma, dma((zn - 1,)), dma((zn - 1,)), dma((7,)), dma((7,)),
        ],
        compiler_params=pltpu.CompilerParams(
            collective_id=0, has_side_effects=True, vmem_limit_bytes=60 * 1024 * 1024),
        cost_estimate=pl.CostEstimate(flops=2 * table_rows * samples * width, bytes_accessed=12 << 20, transcendentals=0),
        name="observe",
    )(traces, table, ids, valid, owner)


def grid_tables():
    index = np.arange(256)
    a, b = index // 16, index % 16
    phase = (a[:, None] * a[None, :] + b[:, None] * b[None, :]) % 16
    angle = 2.0 * np.pi * phase / 16.0
    cos, sin = np.cos(angle), np.sin(angle)
    forward = np.block([[cos, sin], [-sin, cos]]).astype(np.float32)
    inverse = np.block([[cos, -sin], [sin, cos]]).astype(np.float32)
    both = []
    for m in (forward, inverse):
        hi = m.astype(BF16)
        lo = (m - hi.astype(np.float32)).astype(BF16)
        both.append(np.stack([hi, lo]))
    return np.stack(both)


def split(value):
    hi = value.astype(BF16)
    return hi, (value - hi.astype(F32)).astype(BF16)


def mwni_kernel(sum_ref, cnt_ref, tab_ref, out_ref):
    n = 256

    def grid(ref):
        return jnp.concatenate([ref[pl.ds(0, n, stride=2), :], ref[pl.ds(1, n, stride=2), :]], axis=1)

    def left_dot(m, value):
        hi, lo = split(value)
        t_hi, t_lo = tab_ref[m, 0], tab_ref[m, 1]
        dot = functools.partial(jnp.dot, preferred_element_type=F32)
        return dot(t_hi, hi) + (dot(t_hi, lo) + dot(t_lo, hi))

    def right_dot(m, value):
        hi, lo = split(value)
        t_hi, t_lo = tab_ref[m, 0], tab_ref[m, 1]
        dot = functools.partial(jnp.dot, preferred_element_type=F32)
        return dot(hi, t_hi) + (dot(lo, t_hi) + dot(hi, t_lo))

    def transform(forward, re, im):
        mid = left_dot(0 if forward else 1, jnp.concatenate([re, im], axis=0))
        out = right_dot(1 if forward else 0, jnp.concatenate([mid[:n], mid[n:]], axis=1))
        return out[:, :n], out[:, n:]

    count = grid(cnt_ref)
    cover = jnp.minimum(count, 1.0)
    scale = 1.0 / jnp.maximum(count, 1.0)
    obs_re = grid(sum_ref.at[0]) * scale
    obs_im = grid(sum_ref.at[1]) * scale
    re, im = obs_re, obs_im
    cells = n * n
    for step in range(ITERS):
        u_re = cover * obs_re + (1.0 - cover) * re
        u_im = cover * obs_im + (1.0 - cover) * im
        f_re, f_im = transform(True, u_re, u_im)
        power = f_re * f_re + f_im * f_im
        lam = 0.5 * (jnp.sum(power) / cells) + 1e-06
        keep = power / (power + lam)
        re, im = transform(False, f_re * keep, f_im * keep)
        re, im = re * (1.0 / cells), im * (1.0 / cells)
    out_ref[0] = re
    out_ref[1] = im


def mwni(sums, counts, tables):
    vmem = pl.BlockSpec(memory_space=pltpu.VMEM)
    return pl.pallas_call(
        mwni_kernel,
        out_shape=jax.ShapeDtypeStruct((2, 256, 256), F32),
        in_specs=[vmem] * 3,
        out_specs=vmem,
        compiler_params=pltpu.CompilerParams(vmem_limit_bytes=56 * 1024 * 1024),
        name="mwni",
    )(sums, counts, tables)


def local(zn, table, tables, traces, bin_ids, valid, tile_owner):
    tiles = tile_owner.shape[0]
    sums, counts = observe(zn, traces, table, bin_ids.reshape(tiles, TILE), valid.reshape(tiles, TILE), tile_owner)
    state = mwni(sums, counts.reshape(-1, TILE), tables)
    return state.reshape(1, 2, -1)


def solution(mesh):
    zn = mesh.shape["bins"] // YN
    table = dft_table(zn, 250)
    tables = grid_tables()
    in_specs = (P("freq", "bins"), P("bins"), P("bins"), P("bins", None))
    out_specs = P(("bins", "freq"), None, None)

    def run(traces, bin_ids, valid, tile_owner):
        return jax.shard_map(
            functools.partial(local, zn, jnp.asarray(table), jnp.asarray(tables)),
            mesh=mesh, in_specs=in_specs, out_specs=out_specs, check_vma=False,
        )(traces, bin_ids, valid, tile_owner)

    return run
```

time: 804 us -> 189 us (0.24)
  waiting for transfers between devices: 278 us -> 0 us
  other arithmetic: 234 us -> 0 us
  Pallas kernels: 0 us -> 184 us
  blocking collectives: 119 us -> 0 us
  matrix products: 55.5 us -> 0 us
  starting transfers between devices: 49.8 us -> 0 us
  local copies, waits for them, and re-layouts: 45.2 us -> 3.54 us
  between operations: 15.6 us -> 0.01 us
    all_to_all x3 -> x0, waiting for transfers between devices: 244 us -> none  [the longest x1 244 us: local(): lax.all_to_all(data_buf.reshape(span, owners, capacity * tile_len), 'bins...]
    scatter-add x2 -> x0, other arithmetic: 208 us -> none  [the longest x1 104 us: local(): jax.ops.segment_sum(jnp.ones(flat_labels.shape, jnp.float32), flat_labels...]
    pallas_call x0 -> x2, Pallas kernels: none -> 184 us  [the longest x1 174 us: observe(): pl.pallas_call(functools.partial(observe_kernel, zn), out_shape=(jax.Shap...]
    all_gather x1 -> x0, blocking collectives: 119 us -> none  [local(): lax.all_gather(jnp.minimum(count, 1.0).astype(jnp.bfloat16), 'bins', axis...]
    dot_general x33 -> x0, matrix products: 55.5 us -> none  [the longest x32 52.7 us: exact_dot(): jnp.dot(left, right, precision=lax.Precision.HIGHEST, preferred_element_t...]
    all_to_all x3 -> x0, starting transfers between devices: 49.6 us -> none  [the longest x1 18.7 us: local(): lax.all_to_all(label_buf.reshape(1, owners, capacity * tile_len), 'bins',...]
    reduce_scatter x1 -> x0, waiting for transfers between devices: 34 us -> none  [local(): lax.psum_scatter(part.reshape(lax.axis_size('freq') * per_group, 2, local...]
    scatter x2 -> x0, local copies, waits for them, and re-layouts: 23.8 us -> none  [local(): data_buf = jnp.zeros((span, owners * capacity, tile_len), jnp.bfloat16).a...]
  transfers between devices with their start and end apart: 4 -> 0, of which waited for: 2 -> 0; matrix products, arithmetic and copies ran while one was open for 20% -> 0% of each run, Pallas kernels for 0% -> 0%
where the time goes in v2:
time: 189 us; the launch traced here: 187 us
  Pallas kernels  184 us (97%)
  local copies, waits for them, and re-layouts  3.54 us (2%)
    pallas_call x1, Pallas kernels, observe(): pl.pallas_call(functools.partial(observe_kernel, zn), out_shape=(jax.Shap...  174 us
    pallas_call x1, Pallas kernels, mwni(): pl.pallas_call(mwni_kernel, out_shape=jax.ShapeDtypeStruct((2, 256, 256),...  9.92 us

profile of v2, /device:TPU:6, one launch (start us, length us, event | category | flops | bytes accessed | tf_op | source)
XLA Modules:
  0.0 187.1 jit_solution(7168097111130888479)
XLA Ops:
  0.0 1.4 copy.7.owner_ref
  1.4 173.6 %observe.1 = (f32[2,512,128]{2,1,0:T(8,128)}, f32[32,16,128]{2,1,0:T(8,128)}) custom-call(bf16[250,8192]{1,0:T(8,128)(2,1)} %x_hbm.1, bf16[8,1024,250]{2,1,0:T(8,128)(2,1)} %constant.4.clone.tab_hbm, s32[64,128]{1,0:T(8,128)} %bitcast.4, s32[64,128]{1,0:T(8,128)} %bitcast.5, s32[64,1]{1,0:T(8,128)} %copy.7.owner_ref), custom_call_target="tpu_custom_call" | custom-call | flops 4194304000 | bytes 12582912 | tf_op jit(solution)/shard_map/observe/pallas_call | solution.py:409
  175.0 9.9 %mwni.1 = f32[2,256,256]{2,1,0:T(8,128)} custom-call(f32[2,512,128]{2,1,0:T(8,128)} %get-tuple-element.7.sum_ref, f32[512,128]{1,0:T(8,128)} %bitcast.3, bf16[2,2,512,512]{3,2,1,0:T(8,128)(2,1)} %constant.5.clone.tab_ref), custom_call_target="tpu_custom_call" | custom-call | tf_op jit(solution)/shard_map/mwni/pallas_call | solution.py:520
  184.9 2.2 %reshape.15 = f32[1,2,65536]{2,1,0:T(2,128)} reshape(f32[2,256,256]{2,1,0:T(8,128)} %mwni.1) | data formatting | bytes 1048576 | tf_op jit(solution)/shard_map/reshape | solution.py:534

commit v3 on v2

--- a/solution.py
+++ b/solution.py
@@ -19,6 +19,7 @@
 NQ = 8
 BF_STEPS = 6
 NJ = 4
+UNROLL = 8
 F32 = jnp.float32
 BF16 = jnp.bfloat16
 
@@ -40,7 +41,7 @@
 
 
 def observe_kernel(zn, x_hbm, tab_hbm, ids_ref, valid_ref, owner_ref, out_ref, tot_ref,
-                   xm, tab, far_out, far_l, far_r, near_r_out, near_l_out, near_l, near_r, fin,
+                   xm, tab, far_out, far_l, far_r, near_r_out, near_l_out, near_l, near_r, fin, early,
                    plane0, plane1, acc0, acc1, cnt, pay, labs, slots, rb, sb, rf, sf, cz,
                    tab_sem, loc_sem, core_send, core_recv, far_send, far_recv, near_send, near_recv,
                    y_send, y_recv, own_sem, lab_send, lab_recv, lab_own, slot_sem,
@@ -55,6 +56,7 @@
     blk = tab.shape[1] // XN // 2
     part = blk // (YN * CN)
     tiles = ids_ref.shape[0]
+    owners = zn * YN
     hops = zn // 2
     rows = acc0.shape[1]
     nj = NJ
@@ -73,7 +75,6 @@
     def along_z(dz):
         return (lax.rem(z + dz, zn) * YN + y, freq)
 
-    nexts = (along_z(1), along_z(zn - 1))
     peers = [(dy, dc) for dy in range(YN) for dc in range(CN) if (dy, dc) != (0, 0)]
     x_peer = [(bins, lax.rem(x + dx, XN) * CN + c) for dx in range(1, XN)]
     y_peer = [plane(dy, 0) for dy in range(1, YN)]
@@ -106,21 +107,21 @@
         pl.semaphore_signal(barrier, inc=1, device_id=device, device_id_type=MESH)
     pl.semaphore_signal(barrier, inc=1, device_id=x_peer[1], device_id_type=MESH)
 
-    @pl.loop(1, zn)
-    def _(dz):
-        pl.semaphore_signal(barrier, inc=1, device_id=along_z(dz), device_id_type=MESH)
+    for side in (0, 1):
+        pl.semaphore_signal(barrier, inc=1, device_id=along_z(1 + side * (zn - 2)), device_id_type=MESH)
 
     pay[:tiles] = jnp.where(valid_ref[...] > 0, ids_ref[...], LB)
-    tile_no = lax.broadcasted_iota(jnp.int32, (tiles, TILE), 0)
-    named = owner_ref[...] == lax.broadcasted_iota(jnp.int32, (tiles, TILE), 1)
-    none = tiles + 2
-    first = jnp.min(jnp.where(named, tile_no, none), axis=0, keepdims=True)
-    second = jnp.max(jnp.where(named, tile_no, -1), axis=0, keepdims=True)
+    tile_no = lax.broadcasted_iota(jnp.int32, (owners, tiles), 1)
+    named = owner_ref[...] == lax.broadcasted_iota(jnp.int32, (owners, tiles), 0)
+    none = tiles + owners
+    first = jnp.min(jnp.where(named, tile_no, none), axis=1, keepdims=True)
+    second = jnp.max(jnp.where(named, tile_no, -1), axis=1, keepdims=True)
     second = jnp.where(second > first, second, none)
-    tail_row = lax.broadcasted_iota(jnp.int32, (8, TILE), 0)
-    pay[tiles:tiles + 8] = jnp.where(tail_row == 0, first, jnp.where(tail_row == 1, second, LB))
-
-    pl.semaphore_wait(barrier, 3 + len(peers) + zn - 1)
+    lane = lax.broadcasted_iota(jnp.int32, (owners, TILE), 1)
+    pay[tiles:none] = jnp.where(lane == 0, first, jnp.where(lane == 1, second, LB))
+    pay[none:] = jnp.full((8, TILE), LB, jnp.int32)
+
+    pl.semaphore_wait(barrier, 5 + len(peers))
 
     @pl.loop(0, nq)
     def _(q):
@@ -167,8 +168,8 @@
 
     def near_step(h, q):
         hq = h * nq + q
-        to_right = product(h, lax.rem(x + 1, XN), q)
-        to_left = product(h, lax.rem(x + XN - 1, XN), q)
+        to_right = early[0, q] if h else product(h, lax.rem(x + 1, XN), q)
+        to_left = early[1, q] if h else product(h, lax.rem(x + XN - 1, XN), q)
         mid = blk // 2
         far_copy(hq, 0).wait_recv()
         near_r_out[hq, :mid] = (to_right[:mid] + far_l[hq].astype(F32)).astype(BF16)
@@ -181,7 +182,7 @@
 
     def final_step(h, q):
         hq = h * nq + q
-        mine = product(h, x, q)
+        mine = early[2, q] if h else product(h, x, q)
         near_copy(hq, 0).wait_recv()
         near_copy(hq, 1).wait_recv()
         full = (mine + (near_l[hq].astype(F32) + near_r[hq].astype(F32))).astype(BF16)
@@ -199,7 +200,7 @@
         lefts, rights = [], []
         for yy in range(YN):
             for rank in range(2):
-                t = slots[yy, rank, o]
+                t = jnp.clip(slots[yy, o, rank], 0, none)
                 label = labs[yy, pl.ds(t, 1), :]
                 tv = jnp.minimum(t, tiles - 1)
                 vals = spectra[h][yy * (tiles // per_chunk) + tv // per_chunk, tv % per_chunk]
@@ -218,20 +219,24 @@
             cnt[where, :] = sums[HIGH * part: HIGH * part + HIGH]
 
     def bin_range(h, j):
-        owners = per // HIGH
-
-        @pl.loop(j * owners, (j + 1) * owners)
-        def _(o):
-            bin_owner(h, o)
+        count = per // HIGH
+
+        @pl.loop(0, count, step=UNROLL)
+        def _(k):
+            for u in range(UNROLL):
+                bin_owner(h, j * count + k + u)
+
+    def next_z(side):
+        return along_z(1 + side * (zn - 2))
 
     def b_copy(h, side, s, j):
         return remote(sb.at[h, side, s, j], rb.at[h, side, s, j],
-                      b_send.at[h, side, s, j], b_recv.at[h, side, s, j], nexts[side])
+                      b_send.at[h, side, s, j], b_recv.at[h, side, s, j], next_z(side))
 
     def f_copy(h, side, s, j):
         k = s - BF_STEPS
         return remote(sf.at[h, side, k, j], rf.at[h, side, k, j],
-                      f_send.at[h, side, k, j], f_recv.at[h, side, k, j], nexts[side])
+                      f_send.at[h, side, k, j], f_recv.at[h, side, k, j], next_z(side))
 
     def z_send(h, side, s, j, value):
         if s < BF_STEPS:
@@ -248,29 +253,54 @@
         f_copy(h, side, s, j).wait_recv()
         return rf[h, side, s - BF_STEPS, j]
 
-    def first_side(j):
-        return 0 if j < nj // 2 else 1
-
-    def z_item(h, s, j):
-        span = slice(j * per, (j + 1) * per)
-        if s == 0:
+    def own_bins(h, side, s, j):
+        dest = lax.rem(z + hops - s + side * (2 * s), zn)
+        return accs[h][dest, pl.ds(pl.multiple_of(j * per, per), per), :]
+
+    def z_second(h, j):
+        side = j // (nj // 2)
+        z_send(h, side, 1, j, own_bins(h, side, 1, j) + z_take(h, side, 0, j))
+        z_send(h, 1 - side, 1, j, own_bins(h, 1 - side, 1, j))
+
+    def z_first_steps(h):
+        @pl.loop(0, nj)
+        def _(j):
             bin_range(h, j)
-            z_send(h, first_side(j), 0, j, accs[h][lax.rem(z + hops, zn), span, :])
-        elif s < hops:
+            side = j // (nj // 2)
+            z_send(h, side, 0, j, own_bins(h, side, 0, j))
+
+            @pl.when(j > 0)
+            def _():
+                z_second(h, j - 1)
+
+        z_second(h, nj - 1)
+
+    def z_step(h, s, beside=None):
+        @pl.loop(0, nj)
+        def _(j):
             for side in (0, 1):
-                dest = lax.rem(z + hops - s, zn) if side == 0 else lax.rem(z + zn - hops + s, zn)
-                value = accs[h][dest, span, :]
-                if s > 1 or side == first_side(j):
-                    value = value + z_take(h, side, s - 1, j)
-                z_send(h, side, s, j, value)
-        else:
+                z_send(h, side, s, j, own_bins(h, side, s, j) + z_take(h, side, s - 1, j))
+            if beside is not None:
+                beside(j)
+
+    def z_final(h):
+        @pl.loop(0, nj)
+        def _(j):
             value = z_take(h, 0, hops - 1, j) + z_take(h, 1, hops - 1, j)
-            out_ref[h, span, :] = value + accs[h][z, span, :]
+            out_ref[h, pl.ds(pl.multiple_of(j * per, per), per), :] = value + own_bins(h, 0, hops, j)
 
     mine_rows = pl.ds(pl.multiple_of(place * crow, crow), crow)
 
-    def cz_copy(dz):
-        return remote(cnt.at[mine_rows], cz.at[z], cz_send.at[dz - 1], cz_recv.at[dz - 1], along_z(dz))
+    def cz_copy(hop, side):
+        slot = lax.rem(z + zn + (2 * side - 1) * (hop - 1), zn)
+        return remote(cz.at[slot], cz.at[slot], cz_send.at[side, hop - 1], cz_recv.at[side, hop - 1], next_z(side))
+
+    def counts_onward(hop):
+        if hop > 1:
+            for side in (0, 1):
+                cz_copy(hop - 1, side).wait_recv()
+        for side in ((0, 1) if hop < hops else (0,)):
+            cz_copy(hop, side).start()
 
     cnt_own = pltpu.make_async_copy(cnt.at[mine_rows], cz.at[z], cz_own)
 
@@ -292,6 +322,12 @@
         core_arrival(q).wait_recv()
         far_step(0, q)
 
+    for dy in range(1, YN):
+        lab_copy(dy).wait()
+    lab_local.wait()
+    slot_copy = pltpu.make_async_copy(labs.at[:, pl.ds(tiles, owners)], slots, slot_sem)
+    slot_copy.start()
+
     @pl.loop(0, nq)
     def _(q):
         near_step(0, q)
@@ -300,12 +336,10 @@
     def _(q):
         final_step(0, q)
         far_step(1, q)
-
-    for dy in range(1, YN):
-        lab_copy(dy).wait()
-    lab_local.wait()
-    slot_copy = pltpu.make_async_copy(labs.at[:, pl.ds(tiles, 8)], slots, slot_sem)
-    slot_copy.start()
+        early[0, q] = product(1, lax.rem(x + 1, XN), q)
+        early[1, q] = product(1, lax.rem(x + XN - 1, XN), q)
+        early[2, q] = product(1, x, q)
+
     slot_copy.wait()
 
     def plane_arrived(h):
@@ -316,51 +350,64 @@
             own_copy(h, q).wait()
 
     plane_arrived(0)
-    lag = hops
-    pair = max(1, nq // 4)
-    near_at, final_at = 2, 5
-    for d in range(lag + hops + nj):
-        for j in range(nj):
-            if 0 <= d - j <= hops:
-                z_item(0, d - j, j)
-        if near_at <= d < near_at + nq // pair:
-            @pl.loop((d - near_at) * pair, (d - near_at + 1) * pair)
-            def _(q):
-                near_step(1, q)
-        if final_at <= d < final_at + nq // pair:
-            @pl.loop((d - final_at) * pair, (d - final_at + 1) * pair)
-            def _(q):
-                final_step(1, q)
-        if d == lag:
-            plane_arrived(1)
-        for j in range(nj):
-            if 0 <= d - lag - j <= hops:
-                z_item(1, d - lag - j, j)
-        if d == nj:
-            cnt_own.start()
-
-            @pl.loop(1, zn)
-            def _(dz):
-                cz_copy(dz).start()
-        if d == nj + 3:
-            @pl.loop(1, zn)
-            def _(dz):
-                cz_copy(dz).wait()
-            cnt_own.wait()
-            tot_ref[pl.ds(place, 1)] = jnp.sum(cz[...], axis=0)[None]
-            for args in stages[0]:
-                gather(*args).start()
-        if d == nj + 5:
-            for args in stages[0]:
-                gather(*args).wait()
-            for args in stages[1]:
-                gather(*args).start()
-        if d == nj + 7:
-            for args in stages[1]:
-                gather(*args).wait()
-            for args in stages[2]:
-                gather(*args).start()
-
+    z_first_steps(0)
+    cnt_own.start()
+    cnt_own.wait()
+    counts_onward(1)
+
+    quarter = nq // (2 * nj)
+
+    def near_beside(first):
+        def work(j):
+            for i in range(quarter):
+                near_step(1, first + j * quarter + i)
+        return work
+
+    def final_beside(first):
+        def work(j):
+            for i in range(quarter):
+                final_step(1, first + j * quarter + i)
+        return work
+
+    z_step(0, 2, near_beside(0))
+    counts_onward(2)
+    z_step(0, 3, near_beside(nq // 2))
+    counts_onward(3)
+    z_step(0, 4)
+    counts_onward(4)
+    z_step(0, 5)
+    counts_onward(5)
+    z_step(0, 6, final_beside(0))
+    counts_onward(6)
+    z_step(0, 7)
+    counts_onward(7)
+
+    @pl.loop(nq // 2, nq)
+    def _(q):
+        final_step(1, q)
+
+    plane_arrived(1)
+    z_first_steps(1)
+    counts_onward(8)
+    z_final(0)
+    z_step(1, 2)
+    cz_copy(8, 0).wait_recv()
+    tot_ref[pl.ds(place, 1)] = jnp.sum(cz[...], axis=0)[None]
+    for args in stages[0]:
+        gather(*args).start()
+    z_step(1, 3)
+    for args in stages[0]:
+        gather(*args).wait()
+    for args in stages[1]:
+        gather(*args).start()
+    z_step(1, 4)
+    for args in stages[1]:
+        gather(*args).wait()
+    for args in stages[2]:
+        gather(*args).start()
+    for s in range(5, hops):
+        z_step(1, s)
+    z_final(1)
     for args in stages[2]:
         gather(*args).wait()
 
@@ -374,16 +421,24 @@
             for i in range(len(peers)):
                 y_copy(h, q, i).wait_send()
 
-    for h in (0, 1):
-        for s in range(hops):
-            for j in range(nj):
+    for hop in range(1, hops + 1):
+        for side in ((0, 1) if hop < hops else (0,)):
+            cz_copy(hop, side).wait_send()
+
+    @pl.loop(0, nj)
+    def _(j):
+        for h in (0, 1):
+            b_copy(h, j // (nj // 2), 0, j).wait_send()
+
+            @pl.loop(1, BF_STEPS)
+            def _(s):
                 for side in (0, 1):
-                    if s == 0 and side != first_side(j):
-                        continue
-                    if s < BF_STEPS:
-                        b_copy(h, side, s, j).wait_send()
-                    else:
-                        f_copy(h, side, s, j).wait_send()
+                    b_copy(h, side, s, j).wait_send()
+
+            @pl.loop(BF_STEPS, hops)
+            def _(s):
+                for side in (0, 1):
+                    f_copy(h, side, s, j).wait_send()
 
 
 def observe(zn, traces, table, ids, valid, owner):
@@ -397,7 +452,8 @@
     tiles = ids.shape[0]
     hops = zn // 2
     fs = hops - BF_STEPS
-    rows = zn * YN * HIGH
+    owners = zn * YN
+    rows = owners * HIGH
     per = rows // NJ
     places = YN * XN * CN
     crow = rows // places
@@ -425,13 +481,14 @@
             pltpu.VMEM((2 * nq, blk, chunk), BF16),
             pltpu.VMEM((2 * nq, blk, chunk), BF16),
             pltpu.VMEM((2 * nq, chunk // TILE, blk, TILE), BF16),
+            pltpu.VMEM((XN - 1, nq, blk, chunk), F32),
             plane_buf, plane_buf,
             pltpu.VMEM((part, rows, TILE), F32),
             pltpu.VMEM((part, rows, TILE), F32),
             pltpu.VMEM((rows, TILE), F32),
-            pltpu.VMEM((tiles + 8, TILE), jnp.int32),
-            pltpu.VMEM((YN, tiles + 8, TILE), jnp.int32),
-            pltpu.SMEM((YN, 8, TILE), jnp.int32),
+            pltpu.VMEM((tiles + owners + 8, TILE), jnp.int32),
+            pltpu.VMEM((YN, tiles + owners + 8, TILE), jnp.int32),
+            pltpu.SMEM((YN, owners, TILE), jnp.int32),
             pltpu.VMEM((2, 2, BF_STEPS, NJ, per, TILE), BF16),
             pltpu.VMEM((2, 2, BF_STEPS, NJ, per, TILE), BF16),
             pltpu.VMEM((2, 2, fs, NJ, per, TILE), F32),
@@ -442,7 +499,7 @@
             dma((2, npeer, nq)), dma((2, npeer, nq)), dma((2, nq)),
             dma((YN - 1,)), dma((YN - 1,)), dma, dma,
             dma((2, 2, BF_STEPS, NJ)), dma((2, 2, BF_STEPS, NJ)), dma((2, 2, fs, NJ)), dma((2, 2, fs, NJ)),
-            dma, dma((zn - 1,)), dma((zn - 1,)), dma((7,)), dma((7,)),
+            dma, dma((2, hops)), dma((2, hops)), dma((7,)), dma((7,)),
         ],
         compiler_params=pltpu.CompilerParams(
             collective_id=0, has_side_effects=True, vmem_limit_bytes=60 * 1024 * 1024),
@@ -456,15 +513,9 @@
     a, b = index // 16, index % 16
     phase = (a[:, None] * a[None, :] + b[:, None] * b[None, :]) % 16
     angle = 2.0 * np.pi * phase / 16.0
-    cos, sin = np.cos(angle), np.sin(angle)
-    forward = np.block([[cos, sin], [-sin, cos]]).astype(np.float32)
-    inverse = np.block([[cos, -sin], [sin, cos]]).astype(np.float32)
-    both = []
-    for m in (forward, inverse):
-        hi = m.astype(BF16)
-        lo = (m - hi.astype(np.float32)).astype(BF16)
-        both.append(np.stack([hi, lo]))
-    return np.stack(both)
+    both = np.concatenate([np.cos(angle), np.sin(angle)], axis=1).astype(np.float32)
+    hi = both.astype(BF16)
+    return np.stack([hi, (both - hi.astype(np.float32)).astype(BF16)])
 
 
 def split(value):
@@ -474,26 +525,32 @@
 
 def mwni_kernel(sum_ref, cnt_ref, tab_ref, out_ref):
     n = 256
+    cells = n * n
 
     def grid(ref):
         return jnp.concatenate([ref[pl.ds(0, n, stride=2), :], ref[pl.ds(1, n, stride=2), :]], axis=1)
 
-    def left_dot(m, value):
-        hi, lo = split(value)
-        t_hi, t_lo = tab_ref[m, 0], tab_ref[m, 1]
-        dot = functools.partial(jnp.dot, preferred_element_type=F32)
-        return dot(t_hi, hi) + (dot(t_hi, lo) + dot(t_lo, hi))
-
-    def right_dot(m, value):
-        hi, lo = split(value)
-        t_hi, t_lo = tab_ref[m, 0], tab_ref[m, 1]
-        dot = functools.partial(jnp.dot, preferred_element_type=F32)
-        return dot(hi, t_hi) + (dot(lo, t_hi) + dot(hi, t_lo))
-
-    def transform(forward, re, im):
-        mid = left_dot(0 if forward else 1, jnp.concatenate([re, im], axis=0))
-        out = right_dot(1 if forward else 0, jnp.concatenate([mid[:n], mid[n:]], axis=1))
-        return out[:, :n], out[:, n:]
+    t_hi, t_lo = tab_ref[0], tab_ref[1]
+    r_hi = jnp.concatenate([t_hi[:, :n], t_hi[:, n:]], axis=0)
+    r_lo = jnp.concatenate([t_lo[:, :n], t_lo[:, n:]], axis=0)
+    dot = functools.partial(jnp.dot, preferred_element_type=F32)
+
+    def transform(sign, re, im):
+        def left(a, b):
+            low = [b, -a] if sign > 0 else [-b, a]
+            return jnp.concatenate([jnp.concatenate([a, b], axis=1), jnp.concatenate(low, axis=1)], axis=0)
+
+        def right(a, b):
+            first, second = ([a, b], [b, -a]) if sign > 0 else ([a, -b], [b, a])
+            return jnp.concatenate([jnp.concatenate(first, axis=1), jnp.concatenate(second, axis=1)], axis=0)
+
+        (re_hi, re_lo), (im_hi, im_lo) = split(re), split(im)
+        hi, lo = left(re_hi, im_hi), left(re_lo, im_lo)
+        mid = dot(t_hi, hi) + (dot(t_hi, lo) + dot(t_lo, hi))
+        (re_hi, re_lo), (im_hi, im_lo) = split(mid[:, :n]), split(mid[:, n:])
+        hi, lo = right(re_hi, im_hi), right(re_lo, im_lo)
+        out = dot(hi, r_hi) + (dot(lo, r_hi) + dot(hi, r_lo))
+        return out[:n], out[n:]
 
     count = grid(cnt_ref)
     cover = jnp.minimum(count, 1.0)
@@ -501,25 +558,25 @@
     obs_re = grid(sum_ref.at[0]) * scale
     obs_im = grid(sum_ref.at[1]) * scale
     re, im = obs_re, obs_im
-    cells = n * n
     for step in range(ITERS):
         u_re = cover * obs_re + (1.0 - cover) * re
         u_im = cover * obs_im + (1.0 - cover) * im
-        f_re, f_im = transform(True, u_re, u_im)
+        f_re, f_im = transform(1, u_re, u_im)
         power = f_re * f_re + f_im * f_im
         lam = 0.5 * (jnp.sum(power) / cells) + 1e-06
         keep = power / (power + lam)
-        re, im = transform(False, f_re * keep, f_im * keep)
+        re, im = transform(-1, f_re * keep, f_im * keep)
         re, im = re * (1.0 / cells), im * (1.0 / cells)
-    out_ref[0] = re
-    out_ref[1] = im
+    for part, value in enumerate((re, im)):
+        for side in range(2):
+            out_ref[pl.ds(2 * side + part, n, stride=4), :] = value[:, side * TILE:(side + 1) * TILE]
 
 
 def mwni(sums, counts, tables):
     vmem = pl.BlockSpec(memory_space=pltpu.VMEM)
     return pl.pallas_call(
         mwni_kernel,
-        out_shape=jax.ShapeDtypeStruct((2, 256, 256), F32),
+        out_shape=jax.ShapeDtypeStruct((1024, TILE), F32),
         in_specs=[vmem] * 3,
         out_specs=vmem,
         compiler_params=pltpu.CompilerParams(vmem_limit_bytes=56 * 1024 * 1024),
@@ -529,9 +586,10 @@
 
 def local(zn, table, tables, traces, bin_ids, valid, tile_owner):
     tiles = tile_owner.shape[0]
-    sums, counts = observe(zn, traces, table, bin_ids.reshape(tiles, TILE), valid.reshape(tiles, TILE), tile_owner)
+    sums, counts = observe(zn, traces, table, bin_ids.reshape(tiles, TILE), valid.reshape(tiles, TILE),
+                           tile_owner.reshape(1, tiles))
     state = mwni(sums, counts.reshape(-1, TILE), tables)
-    return state.reshape(1, 2, -1)
+    return state.reshape(-1, 2, TILE).transpose(1, 0, 2).reshape(1, 2, -1)
 
 
 def solution(mesh):

time: 189 us -> 154 us (0.81)
  Pallas kernels: 184 us -> 153 us
  local copies, waits for them, and re-layouts: 3.54 us -> 0 us
    pallas_call x1, Pallas kernels: 174 us -> 145 us  [observe(): pl.pallas_call(functools.partial(observe_kernel, zn), out_shape=(jax.Shap...]
    reshape x1 -> x0, local copies, waits for them, and re-layouts: 2.19 us -> none  [local(): return state.reshape(1, 2, -1)]
where the time goes in v3:
time: 154 us; the launch traced here: 153 us
  Pallas kernels  153 us (99%)
    pallas_call x1, Pallas kernels, observe(): pl.pallas_call(functools.partial(observe_kernel, zn), out_shape=(jax.Shap...  145 us
    pallas_call x1, Pallas kernels, mwni(): pl.pallas_call(mwni_kernel, out_shape=jax.ShapeDtypeStruct((1024, TILE),...  8.73 us

profile of v3, /device:TPU:6, one launch (start us, length us, event | category | flops | bytes accessed | tf_op | source)
XLA Modules:
  0.0 153.3 jit_solution(7404205678359223345)
XLA Ops:
  0.0 144.6 %observe.1 = (f32[2,512,128]{2,1,0:T(8,128)}, f32[32,16,128]{2,1,0:T(8,128)}) custom-call(bf16[250,8192]{1,0:T(8,128)(2,1)} %x_hbm.1, bf16[8,1024,250]{2,1,0:T(8,128)(2,1)} %constant.4.clone.tab_hbm, s32[64,128]{1,0:T(8,128)} %bitcast.10, s32[64,128]{1,0:T(8,128)} %bitcast.11, s32[1,64]{1,0:T(1,128)} %bitcast.12), custom_call_target="tpu_custom_call" | custom-call | flops 4194304000 | bytes 12582912 | tf_op jit(solution)/shard_map/observe/pallas_call | solution.py:465
  144.6 8.7 %mwni.1 = f32[1024,128]{1,0:T(8,128)} custom-call(f32[2,512,128]{2,1,0:T(8,128)} %get-tuple-element.7.sum_ref, f32[512,128]{1,0:T(8,128)} %bitcast.9, bf16[2,256,512]{2,1,0:T(8,128)(2,1)} %constant.5.clone.tab_ref), custom_call_target="tpu_custom_call" | custom-call | tf_op jit(solution)/shard_map/mwni/pallas_call | solution.py:577

commit v4 on v3

--- a/solution.py
+++ b/solution.py
@@ -17,7 +17,7 @@
 XN = 4
 CN = 2
 NQ = 8
-BF_STEPS = 6
+BF_STEPS = 7
 NJ = 4
 UNROLL = 8
 F32 = jnp.float32
@@ -332,6 +332,35 @@
     def _(q):
         near_step(0, q)
 
+    def chunk_arrived(h, q):
+        for i in range(len(peers)):
+            y_copy(h, q, i).wait_recv()
+        own_copy(h, q).wait()
+
+    def plane_arrived(h, first, last):
+        @pl.loop(first, last)
+        def _(q):
+            chunk_arrived(h, q)
+
+    def x_sent(h, q):
+        for side in (0, 1):
+            far_copy(h * nq + q, side).wait_send()
+            near_copy(h * nq + q, side).wait_send()
+        for i in range(len(peers)):
+            y_copy(h, q, i).wait_send()
+
+    def z_sent(h, j, first, last):
+        @pl.loop(first, min(last, BF_STEPS))
+        def _(s):
+            for side in (0, 1):
+                b_copy(h, side, s, j).wait_send()
+
+        if last > BF_STEPS:
+            @pl.loop(BF_STEPS, last)
+            def _(s):
+                for side in (0, 1):
+                    f_copy(h, side, s, j).wait_send()
+
     @pl.loop(0, nq)
     def _(q):
         final_step(0, q)
@@ -340,16 +369,13 @@
         early[1, q] = product(1, lax.rem(x + XN - 1, XN), q)
         early[2, q] = product(1, x, q)
 
+        @pl.when(q >= 2)
+        def _():
+            chunk_arrived(0, q - 2)
+
     slot_copy.wait()
 
-    def plane_arrived(h):
-        @pl.loop(0, nq)
-        def _(q):
-            for i in range(len(peers)):
-                y_copy(h, q, i).wait_recv()
-            own_copy(h, q).wait()
-
-    plane_arrived(0)
+    plane_arrived(0, nq - 2, nq)
     z_first_steps(0)
     cnt_own.start()
     cnt_own.wait()
@@ -382,11 +408,15 @@
     z_step(0, 7)
     counts_onward(7)
 
-    @pl.loop(nq // 2, nq)
+    @pl.loop(0, nq // 2)
     def _(q):
-        final_step(1, q)
-
-    plane_arrived(1)
+        final_step(1, nq // 2 + q)
+        for k in (0, 1):
+            core_copy(2 * q + k).wait_send()
+            x_sent(0, 2 * q + k)
+        chunk_arrived(1, q)
+
+    plane_arrived(1, nq // 2, nq)
     z_first_steps(1)
     counts_onward(8)
     z_final(0)
@@ -405,40 +435,31 @@
         gather(*args).wait()
     for args in stages[2]:
         gather(*args).start()
-    for s in range(5, hops):
-        z_step(1, s)
+    def x_sent_beside(first):
+        def work(j):
+            for i in range(quarter):
+                x_sent(1, first + j * quarter + i)
+        return work
+
+    def z_sent_early(j):
+        b_copy(0, j // (nj // 2), 0, j).wait_send()
+        b_copy(1, j // (nj // 2), 0, j).wait_send()
+        z_sent(0, j, 1, hops)
+
+    z_step(1, 5, x_sent_beside(0))
+    z_step(1, 6, x_sent_beside(nq // 2))
+    z_step(1, 7, z_sent_early)
     z_final(1)
+
     for args in stages[2]:
         gather(*args).wait()
-
-    @pl.loop(0, nq)
-    def _(q):
-        core_copy(q).wait_send()
-        for h in (0, 1):
-            for side in (0, 1):
-                far_copy(h * nq + q, side).wait_send()
-                near_copy(h * nq + q, side).wait_send()
-            for i in range(len(peers)):
-                y_copy(h, q, i).wait_send()
-
     for hop in range(1, hops + 1):
         for side in ((0, 1) if hop < hops else (0,)):
             cz_copy(hop, side).wait_send()
 
     @pl.loop(0, nj)
     def _(j):
-        for h in (0, 1):
-            b_copy(h, j // (nj // 2), 0, j).wait_send()
-
-            @pl.loop(1, BF_STEPS)
-            def _(s):
-                for side in (0, 1):
-                    b_copy(h, side, s, j).wait_send()
-
-            @pl.loop(BF_STEPS, hops)
-            def _(s):
-                for side in (0, 1):
-                    f_copy(h, side, s, j).wait_send()
+        z_sent(1, j, 1, hops)
 
 
 def observe(zn, traces, table, ids, valid, owner):

time: 154 us -> 149 us (0.968)
  Pallas kernels: 153 us -> 149 us
    pallas_call x1, Pallas kernels: 145 us -> 140 us  [observe(): pl.pallas_call(functools.partial(observe_kernel, zn), out_shape=(jax.Shap...]
where the time goes in v4:
time: 149 us
  Pallas kernels  149 us (100%)
    pallas_call x1, Pallas kernels, observe(): pl.pallas_call(functools.partial(observe_kernel, zn), out_shape=(jax.Shap...  140 us
    pallas_call x1, Pallas kernels, mwni(): pl.pallas_call(mwni_kernel, out_shape=jax.ShapeDtypeStruct((1024, TILE),...  8.73 us

profile of v4, /device:TPU:6, one launch (start us, length us, event | category | flops | bytes accessed | tf_op | source)
XLA Modules:
  0.0 148.9 jit_solution(5255530440765307882)
XLA Ops:
  0.0 140.1 %observe.1 = (f32[2,512,128]{2,1,0:T(8,128)}, f32[32,16,128]{2,1,0:T(8,128)}) custom-call(bf16[250,8192]{1,0:T(8,128)(2,1)} %x_hbm.1, bf16[8,1024,250]{2,1,0:T(8,128)(2,1)} %constant.4.clone.tab_hbm, s32[64,128]{1,0:T(8,128)} %bitcast.10, s32[64,128]{1,0:T(8,128)} %bitcast.11, s32[1,64]{1,0:T(1,128)} %bitcast.12), custom_call_target="tpu_custom_call" | custom-call | flops 4194304000 | bytes 12582912 | tf_op jit(solution)/shard_map/observe/pallas_call | solution.py:486
  140.1 8.7 %mwni.1 = f32[1024,128]{1,0:T(8,128)} custom-call(f32[2,512,128]{2,1,0:T(8,128)} %get-tuple-element.7.sum_ref, f32[512,128]{1,0:T(8,128)} %bitcast.9, bf16[2,256,512]{2,1,0:T(8,128)(2,1)} %constant.5.clone.tab_ref), custom_call_target="tpu_custom_call" | custom-call | tf_op jit(solution)/shard_map/mwni/pallas_call | solution.py:598
